TPU v7x, 256 devices: a whole 4x4x8 slice. The times are simulated.
256 devices in a mesh: seq: 8 (over z_hi, core), res: 32 (over y, x, z_lo).
Axes of the slice: x: 4, y: 4, z: 8 (z_hi: 4, z_lo: 2; z = z_hi * 2 + z_lo), core: 2. Of those that a mesh axis runs over, the one named last changes fastest.
Arguments:
- homolog_features: bfloat16 [16, 2048, 256], P('seq', 'res'), may hold values from -6 to 6
- couple_features: bfloat16 [2048, 2048, 128], P('res', 'seq'), may hold values from -40 to 40
- result_adjoint: bfloat16 [16, 2048, 256], P('seq', 'res'), may hold values from -6 to 6
- asking_projection: bfloat16 [256, 256], replicated, may hold values from -0.375 to 0.375
- lookup_projection: bfloat16 [256, 256], replicated, may hold values from -0.375 to 0.375
- content_projection: bfloat16 [256, 256], replicated, may hold values from -0.375 to 0.375
- sigmoid_projection: bfloat16 [256, 256], replicated, may hold values from -0.375 to 0.375
- sigmoid_shift_vector: float32 [256], replicated, may hold values from -4 to 4
- couple_to_heads_map: bfloat16 [128, 8], replicated, may hold values from -0.5 to 0.5
- result_projection: bfloat16 [256, 256], replicated, may hold values from -0.375 to 0.375
Outputs:
- homolog_derivative: bfloat16 [16, 2048, 256], P('seq', 'res')
- couple_derivative: bfloat16 [2048, 2048, 128], P('res', 'seq')
All inputs are finite; a program needn't handle non-finite values.
Results may differ from a plain program's by a relative error of at most 0.011.
Values may be sent and summed in bfloat16 or wider, within the bound.
A program may use at most 128 MiB of HBM per device.

v0:
```python
import jax
import jax.numpy as jnp
from jax import lax
from jax.sharding import PartitionSpec as P


def per_device(
    homolog_features,
    couple_features,
    result_adjoint,
    asking_projection,
    lookup_projection,
    content_projection,
    sigmoid_projection,
    sigmoid_shift_vector,
    couple_to_heads_map,
    result_projection,
):
    homolog_amount, line_amount, feature_depth = homolog_features.shape
    head_count = couple_to_heads_map.shape[1]
    inner = asking_projection.shape[1]
    head_size = inner // head_count
    logit_scale = head_size ** (-0.5)
    homolog_table_merged = homolog_features.reshape(-1, feature_depth)
    tiles = jnp.einsum(
        "ijc,ch->hij", couple_features, couple_to_heads_map, preferred_element_type=jnp.float32
    )
    bias_rows = lax.all_gather(tiles, "seq", axis=2, tiled=True)
    query_rows = (
        jnp.dot(homolog_table_merged, asking_projection, preferred_element_type=jnp.float32)
        * logit_scale
    ).astype(jnp.bfloat16)
    query_rows = query_rows.reshape(homolog_amount, line_amount, head_count, head_size)
    gate_values = jax.nn.sigmoid(
        jnp.dot(homolog_table_merged, sigmoid_projection, preferred_element_type=jnp.float32)
        + sigmoid_shift_vector
    )
    gate_values = gate_values.reshape(homolog_amount, line_amount, inner)
    incoming_dimensions = homolog_features.shape
    merged_lines = homolog_features.reshape(-1, feature_depth)
    key_part = jnp.dot(merged_lines, lookup_projection, preferred_element_type=jnp.float32).astype(
        jnp.bfloat16
    )
    value_part = jnp.dot(
        merged_lines, content_projection, preferred_element_type=jnp.float32
    ).astype(jnp.bfloat16)
    both = lax.all_gather(
        jnp.concatenate([key_part, value_part], 1).reshape(
            incoming_dimensions[0], incoming_dimensions[1], 2 * inner
        ),
        "res",
        axis=1,
        tiled=True,
    )
    total = both.shape[1]
    key_rows = both[..., :inner].reshape(homolog_amount, total, head_count, head_size)
    value_rows = both[..., inner:].reshape(homolog_amount, total, head_count, head_size)
    d_gated = jnp.dot(
        result_adjoint.reshape(-1, feature_depth),
        result_projection.T,
        preferred_element_type=jnp.float32,
    )
    d_gated = d_gated.reshape(homolog_amount, line_amount, inner)

    def per_homolog(carry, layer_inputs):
        q_one, k_one, v_one, gate_one, grad_one = layer_inputs
        scores = (
            jnp.einsum("ihd,jhd->hij", q_one, k_one, preferred_element_type=jnp.float32) + bias_rows
        )
        probs = jax.nn.softmax(scores, axis=-1)
        probs_b = probs.astype(jnp.bfloat16)
        attended = jnp.einsum(
            "hij,jhd->ihd", probs_b, v_one, preferred_element_type=jnp.float32
        ).reshape(line_amount, inner)
        d_attended = (grad_one * gate_one).astype(jnp.bfloat16)
        d_gate_pre = (grad_one * attended * gate_one * (1.0 - gate_one)).astype(jnp.bfloat16)
        d_att_heads = d_attended.reshape(line_amount, head_count, head_size)
        d_probs = jnp.einsum("ihd,jhd->hij", d_att_heads, v_one, preferred_element_type=jnp.float32)
        delta = jnp.sum(probs * d_probs, axis=-1, keepdims=True)
        d_scores = probs * (d_probs - delta)
        d_scores_b = d_scores.astype(jnp.bfloat16)
        d_values = jnp.einsum(
            "hij,ihd->jhd", probs_b, d_att_heads, preferred_element_type=jnp.float32
        ).reshape(total, inner)
        d_keys = jnp.einsum(
            "hij,ihd->jhd", d_scores_b, q_one, preferred_element_type=jnp.float32
        ).reshape(total, inner)
        d_query = (
            jnp.einsum("hij,jhd->ihd", d_scores_b, k_one, preferred_element_type=jnp.float32)
            * logit_scale
        )
        d_query = d_query.astype(jnp.bfloat16).reshape(line_amount, inner)
        local_part = jnp.dot(d_query, asking_projection.T, preferred_element_type=jnp.float32)
        local_part = local_part + jnp.dot(
            d_gate_pre, sigmoid_projection.T, preferred_element_type=jnp.float32
        )
        return (carry + d_scores, (local_part, jnp.concatenate([d_keys, d_values], 1)))

    beginning_position = jnp.zeros((head_count, line_amount, total), jnp.float32)
    d_bias_local, (per_chip_pieces, partials) = lax.scan(
        per_homolog, beginning_position, (query_rows, key_rows, value_rows, gate_values, d_gated)
    )
    key_back = jnp.concatenate([lookup_projection.T, content_projection.T], 0).astype(jnp.float32)
    summed = lax.psum_scatter(partials, "res", scatter_dimension=1, tiled=True)
    lookup_derivative = jnp.dot(
        summed.reshape(-1, 2 * inner), key_back, precision=lax.Precision.HIGHEST
    )
    lookup_derivative = lookup_derivative.reshape(homolog_amount, line_amount, feature_depth)
    homolog_derivative = (per_chip_pieces + lookup_derivative).astype(jnp.bfloat16)
    adjoint_for_shift = lax.psum_scatter(d_bias_local, "seq", scatter_dimension=2, tiled=True)
    couple_derivative = jnp.einsum(
        "hij,ch->ijc",
        adjoint_for_shift,
        couple_to_heads_map.astype(jnp.float32),
        precision=lax.Precision.HIGHEST,
    ).astype(jnp.bfloat16)
    return (homolog_derivative, couple_derivative)


def solution(mesh):
    in_specs = (
        P("seq", "res", None),
        P("res", "seq", None),
        P("seq", "res", None),
        P(),
        P(),
        P(),
        P(),
        P(),
        P(),
        P(),
    )
    out_specs = (P("seq", "res", None), P("res", "seq", None))
    return jax.shard_map(
        per_device, mesh=mesh, in_specs=in_specs, out_specs=out_specs, check_vma=False
    )
```

profile of v0, /device:TPU:4, one launch (start us, length us, event | category | flops | bytes accessed | tf_op | source)
XLA Modules:
  0.0 954.5 jit_solution(11193195654174070657)
XLA Ops:
  7.3 4.4 fusion.64
  13.8 54.0 %all-gather.5.cloned.1.call-done = f32[8,64,2048]{2,0,1:T(8,128)} async-done(((f32[8,64,256]{2,0,1:T(8,128)}), f32[8,64,2048]{2,0,1:T(8,128)}) %all-gather.5.cloned.1.call-update) | async-done | bytes 4194320 | tf_op jit(solution)/shard_map/all_gather | solution.py:28
  67.8 6.6 copy.37
  74.3 154.3 %all-gather.3.cloned.1.call-done = bf16[2,2048,512]{2,1,0:T(8,128)(2,1)} async-done(((bf16[2,64,512]{2,1,0:T(8,128)(2,1)}), bf16[2,2048,512]{2,1,0:T(8,128)(2,1)}) %all-gather.3.cloned.1.call-update) | async-done | bytes 4194320 | tf_op jit(solution)/shard_map/all_gather | solution.py:47
  228.6 4.4 fusion.72
  233.1 3.0 copy.34
  236.0 4.0 copy.35
  240.0 244.9 %while.15 = (s32[]{:T(128)}, f32[8,64,2048]{2,1,0:T(8,128)}, f32[2,64,256]{2,1,0:T(8,128)S(1)}, f32[2,2048,512]{2,0,1:T(2,128)}, bf16[2,64,8,32]{1,3,2,0:T(8,128...) while((s32[]{:T(128)}, f32[8,64,2048]{2,1,0:T(8,128)}, ...), condition=%wide.region_4.5_spmd.clone, body=%wide.region_0.4_spmd.clone.sunk | while | flops 575838720 | bytes 102357712 | solution.py:100
  240.2 5.9 fusion.139
  246.1 5.2 multiply_reduce_fusion.2
  251.3 6.4 fusion.140
  257.8 1.7 fusion.147
  259.5 5.3 fusion.146
  264.8 4.6 maximum_bitcast_fusion.4
  269.5 10.9 %copy.56 = f32[1,2048,512]{2,0,1:T(1,128)} copy(f32[1,2048,512]{1,2,0:T(8,128)} %maximum_bitcast_fusion.4) | data formatting | bytes 8388608 | tf_op jit(solution)/shard_map/while/body/jit(dynamic_update_index_in_dim)/dynamic_update_slice | solution.py:100
  280.3 74.7 %dynamic_update_slice.14 = f32[2,2048,512]{2,0,1:T(2,128)} dynamic-update-slice(f32[2,2048,512]{2,0,1:T(2,128)} %get-tuple-element.278, f32[1,2048,512]{2,0,1:T(1,128)} %copy.56, s32[]{:T(128)} %get-tuple-element.275, s32[]{:T(128)} %constant.18.clone.1..sunk, s32[]{:T(128)} %constant.18.clone.1..sunk) | dynamic-update-slice | bytes 8388612 | tf_op jit(solution)/shard_map/while/body/jit(dynamic_update_index_in_dim)/dynamic_update_slice | solution.py:100
  355.1 1.9 fusion.141
  357.1 4.5 fusion.143
  362.1 5.9 fusion.139
  368.0 5.2 multiply_reduce_fusion.2
  373.2 7.6 fusion.140
  380.8 1.7 fusion.147
  382.6 5.3 fusion.146
  387.9 4.6 maximum_bitcast_fusion.4
  392.5 10.9 %copy.56 = f32[1,2048,512]{2,0,1:T(1,128)} copy(f32[1,2048,512]{1,2,0:T(8,128)} %maximum_bitcast_fusion.4) | data formatting | bytes 8388608 | tf_op jit(solution)/shard_map/while/body/jit(dynamic_update_index_in_dim)/dynamic_update_slice | solution.py:100
  403.4 74.7 %dynamic_update_slice.14 = f32[2,2048,512]{2,0,1:T(2,128)} dynamic-update-slice(f32[2,2048,512]{2,0,1:T(2,128)} %get-tuple-element.278, f32[1,2048,512]{2,0,1:T(1,128)} %copy.56, s32[]{:T(128)} %get-tuple-element.275, s32[]{:T(128)} %constant.18.clone.1..sunk, s32[]{:T(128)} %constant.18.clone.1..sunk) | dynamic-update-slice | bytes 8388612 | tf_op jit(solution)/shard_map/while/body/jit(dynamic_update_index_in_dim)/dynamic_update_slice | solution.py:100
  478.1 1.9 fusion.141
  480.2 4.5 fusion.143
  487.4 391.1 %all-reduce.3.cloned.1.call-done = f32[2,2048,512]{2,0,1:T(2,128)} async-done(((f32[2,2048,512]{2,0,1:T(2,128)}), f32[2,2048,512]{2,0,1:T(2,128)}) %all-reduce.3.cloned.1.call-update) | async-done | bytes 8388624
  878.5 1.0 constant_dynamic-slice_fusion.1
  880.4 58.3 %reduce-scatter.2.cloned.1.call-done = f32[8,64,256]{2,1,0:T(8,128)} async-done(((f32[8,64,2048]{2,1,0:T(8,128)}), f32[8,64,256]{2,1,0:T(8,128)}) %reduce-scatter.2.cloned.1.call-update) | async-done | bytes 524304 | tf_op jit(solution)/shard_map/reduce_scatter | solution.py:110
  938.7 9.2 convolution_convert_fusion
  (72 shorter events, 5.6 us)
Async XLA Ops:
  7.2 6.4 copy-start
  7.2 4.6 copy-start.7
  7.2 4.6 copy-start.10
  7.2 4.8 copy-start.8
  7.2 5.7 copy-start.4
  7.2 6.1 copy-start.5
  7.2 6.1 copy-start.14
  7.2 6.3 copy-start.12
  7.3 60.5 %all-gather.5.cloned.1.call-start = ((), (), s32[]{:S(2)}) async-start(), calls=%async_computation.2 | async-start | bytes 4718592 | tf_op jit(solution)/shard_map/all_gather | solution.py:28
  11.7 216.9 %all-gather.3.cloned.1.call-start = ((), (), s32[]{:S(2)}) async-start(), calls=%async_computation.1 | async-start | bytes 4325376 | tf_op jit(solution)/shard_map/all_gather | solution.py:47
  12.8 865.7 %all-reduce.3.cloned.1.call-start = ((), (), s32[]{:S(2)}) async-start(), calls=%async_computation.4 | async-start | bytes 16777216
  233.1 7.0 copy-start.6
  240.0 6.1 copy-start.2
  357.1 4.8 copy-start.3
  361.9 6.1 copy-start.2
  480.2 4.8 copy-start.3
  485.0 0.9 copy-start.9
  485.0 1.0 copy-start.11
  485.0 1.1 copy-start.15
  485.0 453.7 %copy-start.13 = (bf16[128,8]{0,1:T(8,128)(2,1)S(1)}, bf16[128,8]{0,1:T(8,128)(2,1)}, u32[]{:S(2)}) copy-start(bf16[128,8]{0,1:T(8,128)(2,1)} %param.20) | copy-start | bytes 6148
  485.1 453.7 %reduce-scatter.2.cloned.1.call-start = ((), (), s32[]{:S(2)}) async-start(), calls=%async_computation.3 | async-start | bytes 4718592 | tf_op jit(solution)/shard_map/reduce_scatter | solution.py:110
  485.6 462.3 %copy-start.1 = (bf16[256,256]{1,0:T(8,128)(2,1)S(1)}, bf16[256,256]{1,0:T(8,128)(2,1)}, u32[]{:S(2)}) copy-start(bf16[256,256]{1,0:T(8,128)(2,1)} %param.21) | copy-start | bytes 393220
Sparse Core Ops, SparseCore 0:
  11.9 55.8 all-gather.4
  69.6 159.0 all-gather.2
  485.1 393.3 all-reduce.2
  881.5 57.1 reduce-scatter.1
where the time goes:
time: 970 us; the launch traced here: 954 us
  waiting for transfers between devices  658 us (68%)
  local copies, waits for them, and re-layouts  192 us (20%)
  matrix products  65.3 us (7%)
  other arithmetic  24.1 us (2%)
  between operations  14.7 us (2%)
    unnamed x5, waiting for transfers between devices  392 us
    dynamic_update_slice x4, local copies, waits for them, and re-layouts, per_device(): lax.scan(per_homolog, beginning_position, (query_rows, key_rows, value_ro...  171 us
    all_gather x1, waiting for transfers between devices, per_device(): lax.all_gather(jnp.concatenate([key_part, value_part], 1).reshape(incomin...  154 us
    reduce_scatter x1, waiting for transfers between devices, per_device(): lax.psum_scatter(d_bias_local, 'seq', scatter_dimension=2, tiled=True)  58.3 us
    all_gather x1, waiting for transfers between devices, per_device(): bias_rows = lax.all_gather(tiles, 'seq', axis=2, tiled=True)  54 us
  transfers between devices with their start and end apart: 4, of which 4 were waited for; matrix products, arithmetic and copies ran while one was open for 1% of the time, Pallas kernels for 0%

commit v1 on v0

v1 whole, which is shorter than its diff:
```python
import functools

import jax
import jax.numpy as jnp
from jax import lax
from jax.experimental import pallas as pl
from jax.experimental.pallas import tpu as pltpu
from jax.sharding import PartitionSpec as P

F32, BF16 = jnp.float32, jnp.bfloat16
MESH = pl.DeviceIdType.MESH
ORDER = (0, 1, 3, 2)
NT = (((1,), (1,)), ((), ()))
TN = (((0,), (0,)), ((), ()))
VMEM_LIMIT = 60 * 1024 * 1024


def dot(a, b, dims=(((1,), (0,)), ((), ()))):
    return lax.dot_general(a, b, dims, preferred_element_type=F32)


def coords():
    s, r = lax.axis_index("seq"), lax.axis_index("res")
    return (
        lax.div(s, 2),
        lax.rem(s, 2),
        lax.div(r, 8),
        lax.rem(lax.div(r, 2), 4),
        lax.rem(r, 2),
    )


def device(zh, c, y, x, zl):
    return (zh * 2 + c, y * 8 + x * 2 + zl)


def mod4(v):
    return lax.rem(v + 8, 4)


def remote(src, dst, ssem, rsem, dev):
    return pltpu.make_async_remote_copy(
        src_ref=src, dst_ref=dst, send_sem=ssem, recv_sem=rsem, device_id=dev, device_id_type=MESH
    )


def entry_barrier(devices):
    barrier = pltpu.get_barrier_semaphore()
    for dev in devices:
        pl.semaphore_signal(barrier, inc=1, device_id=dev, device_id_type=MESH)
    pl.semaphore_wait(barrier, len(devices))


def slab_partners(zh, c, y, x, zl):
    return (
        [device(mod4(zh + d), c, y, x, zl) for d in (1, 2, 3)]
        + [device(zh, c, mod4(y + d), x, zl) for d in (1, 3)]
        + [device(zh, c, y, mod4(x + d), zl) for d in (1, 3)]
        + [device(zh, c, y, x, 1 - zl)]
    )


def gather_kernel(
    feat, adj, qf, ag, kv, zs, zr, as_, ar, ys, yr, ls, lr, xs, xr, x2s, x2r
):
    zh, c, y, x, zl = coords()
    entry_barrier(slab_partners(zh, c, y, x, zl))
    role = mod4(y - zh)
    jb = x * 2 + zl
    left, right = mod4(x - 1), mod4(x + 1)
    dev_left, dev_right = device(zh, c, y, left, zl), device(zh, c, y, right, zl)
    dev_up, dev_down = device(zh, c, mod4(y + 1), x, zl), device(zh, c, mod4(y - 1), x, zl)
    dev_zl = device(zh, c, y, x, 1 - zl)

    def zcopy(src, dst, ssem, rsem, d):
        return remote(
            src, dst.at[pl.ds(2 * zh, 2)], ssem.at[d - 1], rsem.at[d - 1],
            device(mod4(zh + d), c, y, x, zl),
        )

    def zwait(src, dst, ssem, rsem, d):
        remote(
            src, dst.at[pl.ds(2 * mod4(zh - d), 2)], ssem.at[d - 1], rsem.at[d - 1],
            device(mod4(zh + d), c, y, x, zl),
        ).wait_recv()

    for d in (1, 3, 2):
        zcopy(feat, qf, zs, zr, d).start()
    for d in (1, 3, 2):
        zcopy(adj, ag, as_, ar, d).start()
    qf[pl.ds(2 * zh, 2)] = feat[...]
    ag[pl.ds(2 * zh, 2)] = adj[...]

    def chunk(q):
        return 2 * mod4(zh - ORDER[q])

    def y_first(q, which):
        here = kv.at[pl.ds(chunk(q), 2), jb]
        return remote(
            qf.at[pl.ds(chunk(q), 2)], here, ys.at[q, which], yr.at[q, 0], (dev_up, dev_down)[which]
        )

    def y_half(q, which):
        here = kv.at[chunk(q) + which, jb]
        return remote(here, here, ys.at[q, which], yr.at[q, which], (dev_up, dev_down)[which])

    def z_pair(q):
        here = kv.at[pl.ds(chunk(q), 2), jb]
        return remote(here, here, ls.at[q], lr.at[q], dev_zl)

    def z_pair_in(q):
        here = kv.at[pl.ds(chunk(q), 2), x * 2 + 1 - zl]
        return remote(here, here, ls.at[q], lr.at[q], dev_zl)

    def x_first(q, which, owner):
        here = kv.at[pl.ds(chunk(q), 2), pl.ds(2 * owner, 2)]
        return remote(here, here, xs.at[q, which], xr.at[q, which], (dev_right, dev_left)[which])

    def x_half(q, which, owner):
        here = kv.at[chunk(q) + which, pl.ds(2 * owner, 2)]
        return remote(here, here, x2s.at[q, which], x2r.at[q, which], (dev_right, dev_left)[which])

    def stage_y(q):
        d = ORDER[q]
        if d:
            zwait(feat, qf, zs, zr, d)

        @pl.when(role == 0)
        def _():
            y_first(q, 0).start()
            y_first(q, 1).start()
            kv[pl.ds(chunk(q), 2), jb] = qf[pl.ds(chunk(q), 2)]

        @pl.when(role == 1)
        def _():
            y_first(q, 0).wait_recv()
            y_half(q, 0).start()

        @pl.when(role == 3)
        def _():
            y_first(q, 0).wait_recv()
            y_half(q, 1).start()

        @pl.when(role == 2)
        def _():
            y_half(q, 0).wait_recv()
            y_half(q, 1).wait_recv()

        z_pair(q).start()

    def stage_x(q):
        z_pair_in(q).wait_recv()
        x_first(q, 0, x).start()
        x_first(q, 1, x).start()

    def stage_x2(q):
        x_first(q, 0, left).wait_recv()
        x_half(q, 0, left).start()
        x_first(q, 1, right).wait_recv()
        x_half(q, 1, right).start()

    def stage_end(q):
        x_half(q, 0, mod4(x + 2)).wait_recv()
        x_half(q, 1, mod4(x + 2)).wait_recv()

    for t in range(7):
        for lag, stage in enumerate((stage_y, stage_x, stage_x2, stage_end)):
            if 0 <= t - lag < 4:
                stage(t - lag)

    for d in (1, 3, 2):
        zwait(adj, ag, as_, ar, d)
        zcopy(feat, qf, zs, zr, d).wait_send()
        zcopy(adj, ag, as_, ar, d).wait_send()
    for q in range(4):

        @pl.when(role == 0)
        def _():
            y_first(q, 0).wait_send()
            y_first(q, 1).wait_send()

        @pl.when(role == 1)
        def _():
            y_half(q, 0).wait_send()

        @pl.when(role == 3)
        def _():
            y_half(q, 1).wait_send()

        z_pair(q).wait_send()
        for which in (0, 1):
            x_first(q, which, x).wait_send()
            x_half(q, which, x).wait_send()


def head_mask(rows):
    lane = lax.broadcasted_iota(jnp.int32, (rows, 256), 1)
    return [(lane >= 32 * h) & (lane < 32 * h + 32) for h in range(8)]


def spread_map(rep, out):
    row = lax.broadcasted_iota(jnp.int32, (128, 128), 0)
    wide = rep.astype(F32)
    for i in range(16):
        out[:, i * 128 : (i + 1) * 128] = jnp.where(lax.rem(row, 16) == i, wide, 0.0).astype(BF16)


def attention_kernel(
    pair, qf, ag, kv, wq, wk, wv, wg, bg, wo, wback, rep,
    part, ipart, db,
    bias, dbias, pbuf, dpbuf, kbuf, vbuf, qbd, dabd, fac, sbuf, pb, dsb, wexp, st, stout, stin, ab, dbin,
    bs, br, ss, sr, es, er,
):
    zh, c, y, x, zl = coords()
    other = device(zh, 1 - c, y, x, zl)
    peers = [device(mod4(zh + d), c, y, x, zl) for d in (1, 2, 3)]
    entry_barrier([other] + peers)

    spread_map(rep[...], wexp)
    for g in range(4):
        total = jnp.zeros((128, 256), F32)
        for p in range(8):
            i = 16 * g + 2 * p
            both = jnp.concatenate([pair[i], pair[i + 1]], axis=1)
            total += dot(wexp[:, p * 256 : (p + 1) * 256], both, NT)
        for h in range(8):
            bias[c, h * 64 + 16 * g : h * 64 + 16 * g + 16, :] = total[h * 16 : h * 16 + 16]
    swap = remote(bias.at[c], bias.at[c], bs, br, other)
    swap.start()

    masks = head_mask(64)

    def query_side(n, carry):
        rows = qf[n]
        q = (dot(rows, wq[...]) * (32**-0.5)).astype(BF16)
        gate = jax.nn.sigmoid(dot(rows, wg[...]) + bg[...])
        dg = dot(ag[n], wo[...], NT)
        da = (dg * gate).astype(BF16)
        fac[n] = dg * gate * (1.0 - gate)
        for h in range(8):
            qbd[n, h * 64 : h * 64 + 64, :] = jnp.where(masks[h], q.astype(F32), 0.0).astype(BF16)
            dabd[n, h * 64 : h * 64 + 64, :] = jnp.where(masks[h], da.astype(F32), 0.0).astype(BF16)
        k = dot(kv[n], wk[...]).astype(BF16)
        v = dot(kv[n], wv[...]).astype(BF16)
        kbuf[n] = k
        vbuf[n] = v
        return carry

    lax.fori_loop(0, 8, query_side, 0)
    remote(bias.at[1 - c], bias.at[1 - c], bs, br, other).wait_recv()

    lane = lax.broadcasted_iota(jnp.int32, (64, 128), 1)

    def first(n, carry):
        sbuf[...] = dot(qbd[n], kbuf[n], NT)
        dpbuf[n] = dot(dabd[n], vbuf[n], NT)
        for h in range(8):
            rows = pl.ds(h * 64, 64)
            s0 = sbuf[rows, 0:256] + bias[0, rows, :]
            s1 = sbuf[rows, 256:512] + bias[1, rows, :]
            top = jnp.max(jnp.maximum(s0, s1), axis=1, keepdims=True)
            p0, p1 = jnp.exp(s0 - top), jnp.exp(s1 - top)
            pbuf[n, rows, 0:256] = p0
            pbuf[n, rows, 256:512] = p1
            total = jnp.sum(p0 + p1, axis=1, keepdims=True)
            mixed = jnp.sum(
                p0 * dpbuf[n, rows, 0:256] + p1 * dpbuf[n, rows, 256:512], axis=1, keepdims=True
            )
            old = jnp.where(lane == n, top, st[rows, :])
            old = jnp.where(lane == n + 8, total, old)
            st[rows, :] = jnp.where(lane == n + 16, mixed, old)
        return carry

    st[...] = jnp.zeros_like(st)
    lax.fori_loop(0, 8, first, 0)

    stout[...] = st[...].T[0:24]
    for d in (1, 2, 3):
        remote(stout, stin.at[d - 1], ss.at[d - 1], sr.at[d - 1], peers[d - 1]).start()
    for d in (1, 2, 3):
        remote(stout, stin.at[d - 1], ss.at[d - 1], sr.at[d - 1], peers[d - 1]).wait()
    own_top = stout[0:8]
    tops = [own_top] + [stin[d, 0:8] for d in range(3)]
    top = jnp.maximum(jnp.maximum(tops[0], tops[1]), jnp.maximum(tops[2], tops[3]))
    own_scale = jnp.exp(own_top - top)
    total, mixed = own_scale * stout[8:16], own_scale * stout[16:24]
    for d in range(3):
        scale = jnp.exp(tops[d + 1] - top)
        total += scale * stin[d, 8:16]
        mixed += scale * stin[d, 16:24]
    ab[...] = jnp.concatenate(
        [own_scale / total, mixed / total, jnp.zeros((112, 512), F32)], axis=0
    ).T

    dbias[...] = jnp.zeros_like(dbias)

    def second(n, carry):
        for h in range(8):
            rows = pl.ds(h * 64, 64)
            both = ab[rows, :]
            a = jnp.sum(jnp.where(lane == n, both, 0.0), axis=1, keepdims=True)
            delta = jnp.sum(jnp.where(lane == n + 8, both, 0.0), axis=1, keepdims=True)
            for half in (0, 1):
                cols = slice(half * 256, half * 256 + 256)
                probs = pbuf[n, rows, cols] * a
                pb[rows, cols] = probs.astype(BF16)
                ds = probs * (dpbuf[n, rows, cols] - delta)
                dsb[rows, cols] = ds.astype(BF16)
                dbias[half, rows, :] += ds
        att_all = dot(pb[...], vbuf[n])
        dq_all = dot(dsb[...], kbuf[n])
        att, dq = jnp.zeros((64, 256), F32), jnp.zeros((64, 256), F32)
        for h in range(8):
            att += jnp.where(masks[h], att_all[h * 64 : h * 64 + 64], 0.0)
            dq += jnp.where(masks[h], dq_all[h * 64 : h * 64 + 64], 0.0)
        dq = (dq * (32**-0.5)).astype(BF16)
        dgp = (fac[n] * att).astype(BF16)
        ipart[n] = dot(dq, wq[...], NT) + dot(dgp, wg[...], NT)
        dk = dot(qbd[n], dsb[...], TN).astype(BF16)
        dv = dot(dabd[n], pb[...], TN).astype(BF16)
        part[n] = (dot(dk, wback[0:256], TN) + dot(dv, wback[256:512], TN)).astype(BF16)
        return carry

    lax.fori_loop(0, 8, second, 0)

    back = remote(dbias.at[1 - c], dbin, es, er, other)
    back.start()
    back.wait()
    db[...] = dbias[c] + dbin[...]
    swap.wait_send()


def couple_kernel(db, rep, out, wexp):
    spread_map(rep[...], wexp)
    rows = db[...].reshape(128, 256)
    high = rows.astype(BF16)
    low = (rows - high.astype(F32)).astype(BF16)
    both = jnp.concatenate([high, low], axis=0).T
    for p in range(8):
        w = wexp[:, p * 256 : (p + 1) * 256]
        res = dot(both, jnp.concatenate([w, w], axis=0)).astype(BF16)
        out[2 * p] = res[:, 0:128]
        out[2 * p + 1] = res[:, 128:256]


def reduce_kernel(
    part, ipart, out,
    acc, tosend, in_x2, in_x, in_l, in_y, zout, zin, hop1, hop2, hopl, hopy,
    x2s, x2r, xs, xr, ls, lr, ys, yr, zs, zr,
):
    zh, c, y, x, zl = coords()
    entry_barrier(slab_partners(zh, c, y, x, zl))
    role = mod4(y - zh)
    left, right, far = mod4(x - 1), mod4(x + 1), mod4(x + 2)
    dev_left, dev_right = device(zh, c, y, left, zl), device(zh, c, y, right, zl)
    dev_up, dev_down = device(zh, c, mod4(y + 1), x, zl), device(zh, c, mod4(y - 1), x, zl)
    dev_zl = device(zh, c, y, x, 1 - zl)
    sides = (dev_right, dev_left)
    near = (right, left)

    def chunk(q):
        return 2 * mod4(zh - ORDER[3 - q])

    def x_half(q, which):
        return remote(
            part.at[chunk(q) + which, pl.ds(2 * far, 2)], in_x2.at[q, which],
            x2s.at[q, which], x2r.at[q, which], sides[which],
        )

    def x_first(q, which):
        return remote(
            hop1.at[q, which], in_x.at[q, which], xs.at[q, which], xr.at[q, which], sides[which]
        )

    def z_pair(q):
        return remote(hopl.at[q], in_l.at[q], ls.at[q], lr.at[q], dev_zl)

    def y_half(q, which):
        return remote(
            hopy.at[q, which], in_y.at[q, 0, which], ys.at[q, which], yr.at[q, 0],
            (dev_down, dev_up)[which],
        )

    def y_first(q, which):
        return remote(
            hopy.at[q], in_y.at[q, which], ys.at[q, 0], yr.at[q, which], (dev_down, dev_up)[which]
        )

    def z_out(q):
        d = ORDER[3 - q]
        return remote(
            zout.at[q], zin.at[q], zs.at[q], zr.at[q], device(mod4(zh - d), c, y, x, zl)
        )

    def stage_x(q):
        for which in (0, 1):
            x_half(q, which).start()

    def stage_x2(q):
        for which in (0, 1):
            x_half(q, which).wait_recv()
            n = chunk(q)
            mine = part[pl.ds(n, 2), pl.ds(2 * near[which], 2)].astype(F32)
            got = in_x2[q, which].astype(F32)
            if which == 0:
                hop1[q, which, 0] = (mine[0] + got).astype(BF16)
                hop1[q, which, 1] = mine[1].astype(BF16)
            else:
                hop1[q, which, 0] = mine[0].astype(BF16)
                hop1[q, which, 1] = (mine[1] + got).astype(BF16)
            x_first(q, which).start()

    def stage_l(q):
        for which in (0, 1):
            x_first(q, which).wait_recv()
        n = chunk(q)

        def total(b):
            return (
                part[pl.ds(n, 2), 2 * x + b].astype(F32)
                + in_x[q, 0, :, b].astype(F32)
                + in_x[q, 1, :, b].astype(F32)
            )

        acc[q] = total(zl)
        hopl[q] = total(1 - zl).astype(BF16)
        z_pair(q).start()

    def stage_y(q):
        z_pair(q).wait_recv()
        acc[q] = acc[q] + in_l[q].astype(F32)

        @pl.when(role == 2)
        def _():
            hopy[q] = acc[q].astype(BF16)
            y_half(q, 0).start()
            y_half(q, 1).start()

    def stage_y2(q):
        @pl.when(role == 1)
        def _():
            y_half(q, 0).wait_recv()
            acc[q, 0] = acc[q, 0] + in_y[q, 0, 0].astype(F32)
            hopy[q] = acc[q].astype(BF16)
            y_first(q, 0).start()

        @pl.when(role == 3)
        def _():
            y_half(q, 1).wait_recv()
            acc[q, 1] = acc[q, 1] + in_y[q, 0, 1].astype(F32)
            hopy[q] = acc[q].astype(BF16)
            y_first(q, 1).start()

    def stage_z(q):
        n = chunk(q)
        mine = ipart[pl.ds(n, 2)]

        @pl.when(role == 0)
        def _():
            y_first(q, 0).wait_recv()
            y_first(q, 1).wait_recv()
            acc[q] = (
                mine + acc[q] + in_y[q, 0].astype(F32) + in_y[q, 1].astype(F32)
            )

        @pl.when(role != 0)
        def _():
            acc[q] = mine

        if ORDER[3 - q]:
            zout[q] = acc[q].astype(BF16)
            z_out(q).start()

    for t in range(9):
        for lag, stage in enumerate((stage_x, stage_x2, stage_l, stage_y, stage_y2, stage_z)):
            if 0 <= t - lag < 4:
                stage(t - lag)

    total = acc[3]
    for q in range(3):
        z_out(q).wait_recv()
        total += zin[q].astype(F32)
    out[...] = total.astype(BF16)

    for q in range(4):
        for which in (0, 1):
            x_half(q, which).wait_send()
            x_first(q, which).wait_send()
        z_pair(q).wait_send()

        @pl.when(role == 2)
        def _():
            y_half(q, 0).wait_send()
            y_half(q, 1).wait_send()

        @pl.when(role == 1)
        def _():
            y_first(q, 0).wait_send()

        @pl.when(role == 3)
        def _():
            y_first(q, 1).wait_send()

        if q < 3:
            z_out(q).wait_send()


VM = pl.BlockSpec(memory_space=pltpu.VMEM)
DMA = pltpu.SemaphoreType.DMA


def params(cid):
    return pltpu.CompilerParams(
        collective_id=cid, has_side_effects=True, vmem_limit_bytes=VMEM_LIMIT
    )


def per_device(feat, pair, adj, wq, wk, wv, wg, bg, wch, wo):
    rep = jnp.repeat(wch.T, 16, axis=0)
    wback = jnp.concatenate([wk.T, wv.T], axis=0)
    sds = jax.ShapeDtypeStruct
    qf, ag, kv = pl.pallas_call(
        gather_kernel,
        out_shape=(
            sds((8, 64, 256), BF16), sds((8, 64, 256), BF16), sds((8, 8, 64, 256), BF16)
        ),
        in_specs=[VM] * 2,
        out_specs=(VM,) * 3,
        scratch_shapes=[DMA((3,))] * 4
        + [DMA((4, 2))] * 2 + [DMA((4,))] * 2 + [DMA((4, 2))] * 4,
        compiler_params=params(0),
        name="gather",
    )(feat, adj)
    part, ipart, db = pl.pallas_call(
        attention_kernel,
        out_shape=(sds((8, 512, 256), BF16), sds((8, 64, 256), F32), sds((512, 256), F32)),
        in_specs=[VM] * 12,
        out_specs=(VM,) * 3,
        scratch_shapes=[
            pltpu.VMEM((2, 512, 256), F32),
            pltpu.VMEM((2, 512, 256), F32),
            pltpu.VMEM((8, 512, 512), F32),
            pltpu.VMEM((8, 512, 512), F32),
            pltpu.VMEM((8, 512, 256), BF16),
            pltpu.VMEM((8, 512, 256), BF16),
            pltpu.VMEM((8, 512, 256), BF16),
            pltpu.VMEM((8, 512, 256), BF16),
            pltpu.VMEM((8, 64, 256), F32),
            pltpu.VMEM((512, 512), F32),
            pltpu.VMEM((512, 512), BF16),
            pltpu.VMEM((512, 512), BF16),
            pltpu.VMEM((128, 2048), BF16),
            pltpu.VMEM((512, 128), F32),
            pltpu.VMEM((24, 512), F32),
            pltpu.VMEM((3, 24, 512), F32),
            pltpu.VMEM((512, 128), F32),
            pltpu.VMEM((512, 256), F32),
            DMA, DMA, DMA((3,)), DMA((3,)), DMA, DMA,
        ],
        compiler_params=params(1),
        name="attention",
    )(pair, qf, ag, kv.reshape(8, 512, 256), wq, wk, wv, wg, bg.reshape(1, 256), wo, wback, rep)
    homolog = pl.pallas_call(
        reduce_kernel,
        out_shape=sds((2, 64, 256), BF16),
        in_specs=[VM] * 2,
        out_specs=VM,
        scratch_shapes=[
            pltpu.VMEM((4, 2, 64, 256), F32),
            pltpu.VMEM((8, 128), F32),
            pltpu.VMEM((4, 2, 2, 64, 256), BF16),
            pltpu.VMEM((4, 2, 2, 2, 64, 256), BF16),
            pltpu.VMEM((4, 2, 64, 256), BF16),
            pltpu.VMEM((4, 2, 2, 64, 256), BF16),
            pltpu.VMEM((3, 2, 64, 256), BF16),
            pltpu.VMEM((3, 2, 64, 256), BF16),
            pltpu.VMEM((4, 2, 2, 2, 64, 256), BF16),
            pltpu.VMEM((8, 128), F32),
            pltpu.VMEM((4, 2, 64, 256), BF16),
            pltpu.VMEM((4, 2, 64, 256), BF16),
            DMA((4, 2)), DMA((4, 2)), DMA((4, 2)), DMA((4, 2)),
            DMA((4,)), DMA((4,)), DMA((4, 2)), DMA((4, 2)), DMA((3,)), DMA((3,)),
        ],
        compiler_params=params(2),
        name="reduce",
    )(part.reshape(8, 8, 64, 256), ipart)
    couple = pl.pallas_call(
        couple_kernel,
        out_shape=sds((64, 256, 128), BF16),
        grid=(4,),
        in_specs=[
            pl.BlockSpec((8, 16, 256), lambda g: (0, g, 0)),
            pl.BlockSpec((128, 128), lambda g: (0, 0)),
        ],
        out_specs=pl.BlockSpec((16, 256, 128), lambda g: (g, 0, 0)),
        scratch_shapes=[pltpu.VMEM((128, 2048), BF16)],
        compiler_params=pltpu.CompilerParams(vmem_limit_bytes=VMEM_LIMIT),
        name="couple",
    )(db.reshape(8, 64, 256), rep)
    return homolog, couple


def solution(mesh):
    in_specs = (
        P("seq", "res", None), P("res", "seq", None), P("seq", "res", None),
        P(), P(), P(), P(), P(), P(), P(),
    )
    out_specs = (P("seq", "res", None), P("res", "seq", None))
    return jax.shard_map(
        per_device, mesh=mesh, in_specs=in_specs, out_specs=out_specs, check_vma=False
    )
```

time: 970 us -> 136 us (0.14); the launches traced: 954 us -> 133 us
  waiting for transfers between devices: 658 us -> 0 us
  local copies, waits for them, and re-layouts: 192 us -> 3.94 us
  Pallas kernels: 0 us -> 128 us
  matrix products: 65.3 us -> 0 us
  other arithmetic: 24.1 us -> 0.72 us
  between operations: 14.7 us -> 0.68 us
    unnamed x5 -> x0, waiting for transfers between devices: 392 us -> none
    all_gather x2 -> x0, waiting for transfers between devices: 208 us -> none  [the longest x1 154 us: per_device(): lax.all_gather(jnp.concatenate([key_part, value_part], 1).reshape(incomin...]
    dynamic_update_slice x4 -> x0, local copies, waits for them, and re-layouts: 171 us -> none  [per_device(): lax.scan(per_homolog, beginning_position, (query_rows, key_rows, value_ro...]
    pallas_call x0 -> x4, Pallas kernels: none -> 128 us  [the longest x1 44.3 us: per_device(): pl.pallas_call(gather_kernel, out_shape=(sds((8, 64, 256), BF16), sds((8,...]
    reduce_scatter x1 -> x0, waiting for transfers between devices: 58.3 us -> none  [per_device(): lax.psum_scatter(d_bias_local, 'seq', scatter_dimension=2, tiled=True)]
    dot_general x22 -> x0, matrix products: 53.5 us -> none  [the longest x2 10.7 us: per_homolog(): jnp.einsum('hij,ihd->jhd', probs_b, d_att_heads, preferred_element_type=j...]
    convert_element_type x6 -> x0, other arithmetic: 14.2 us -> none  [the longest x2 14 us: per_homolog(): d_scores_b = d_scores.astype(jnp.bfloat16)]
    sub x2 -> x0, matrix products: 11.8 us -> none  [per_homolog(): probs = jax.nn.softmax(scores, axis=-1)]
  transfers between devices with their start and end apart: 4 -> 0, of which waited for: 4 -> 0; matrix products, arithmetic and copies ran while one was open for 1% -> 0% of each run, Pallas kernels for 0% -> 0%
where the time goes in v1:
time: 136 us; the launch traced here: 133 us
  Pallas kernels  128 us (94%)
  local copies, waits for them, and re-layouts  3.94 us (3%)
    pallas_call x1, Pallas kernels, per_device(): pl.pallas_call(gather_kernel, out_shape=(sds((8, 64, 256), BF16), sds((8,...  44.3 us
    pallas_call x1, Pallas kernels, per_device(): pl.pallas_call(attention_kernel, out_shape=(sds((8, 512, 256), BF16), sds...  40.5 us
    pallas_call x1, Pallas kernels, per_device(): pl.pallas_call(reduce_kernel, out_shape=sds((2, 64, 256), BF16), in_specs...  38.5 us
    pallas_call x1, Pallas kernels, per_device(): pl.pallas_call(couple_kernel, out_shape=sds((64, 256, 128), BF16), grid=(...  4.81 us

profile of v1, /device:TPU:4, one launch (start us, length us, event | category | flops | bytes accessed | tf_op | source)
XLA Modules:
  0.0 133.5 jit_solution(2417659300150739969)
XLA Ops:
  0.6 1.3 broadcast_in_dim.3
  1.9 1.0 copy.12
  2.9 1.0 copy.13
  4.0 0.7 pad_maximum_fusion.wback
  4.7 44.3 %gather.1 = (bf16[8,64,256]{2,1,0:T(8,128)(2,1)}, bf16[8,64,256]{2,1,0:T(8,128)(2,1)}, bf16[8,8,64,256]{3,2,1,0:T(8,128)(2,1)}) custom-call(bf16[2,64,256]{2,1,0:T(8,128)(2,1)} %feat.1, bf16[2,64,256]{2,1,0:T(8,128)(2,1)} %adj.1), custom_call_target="tpu_custom_call" | custom-call | tf_op jit(solution)/shard_map/gather/pallas_call | solution.py:522
  49.0 40.5 %attention.1 = (bf16[8,512,256]{2,1,0:T(8,128)(2,1)}, f32[8,64,256]{2,1,0:T(8,128)}, f32[512,256]{1,0:T(8,128)}) custom-call(bf16[64,256,128]{2,1,0:T(8,128)(2,1)} %pair.1, bf16[8,64,256]{2,1,0:T(8,128)(2,1)} %get-tuple-element.8.qf, bf16[8,64,256]{2,1,0:T(8,128)(2,1)} %get-tuple-element.9.ag, bf16[8,512,256]{2,1,0:T(8,128)(2,1)} %bitcast.9, ...), custom_call_target="tpu_custom_call" | custom-call | tf_op jit(solution)/shard_map/attention/pallas_call | solution.py:534
  89.6 38.5 %reduce.1 = bf16[2,64,256]{2,1,0:T(8,128)(2,1)} custom-call(bf16[8,8,64,256]{3,2,1,0:T(8,128)(2,1)} %bitcast.8, f32[8,64,256]{2,1,0:T(8,128)} %get-tuple-element.12.ipart), custom_call_target="tpu_custom_call" | custom-call | tf_op jit(solution)/shard_map/reduce/pallas_call | solution.py:563
  128.0 0.0 copy-start
  128.1 4.8 %couple.1 = bf16[64,256,128]{2,1,0:T(8,128)(2,1)} custom-call(f32[8,64,256]{2,1,0:T(8,128)} %bitcast.10, bf16[128,128]{1,0:T(8,128)(2,1)} %bitcast.14), custom_call_target="tpu_custom_call" | custom-call | tf_op jit(solution)/shard_map/couple/pallas_call | solution.py:587
  132.9 0.0 copy-done
  132.9 0.6 copy.15
Async XLA Ops:
  128.0 4.8 %copy-start = (bf16[2,64,256]{2,1,0:T(8,128)(2,1)S(1)}, bf16[2,64,256]{2,1,0:T(8,128)(2,1)}, u32[]{:S(2)}) copy-start(bf16[2,64,256]{2,1,0:T(8,128)(2,1)} %reduce.1) | copy-start | bytes 196612

commit v2 on v0

v2 whole, which is shorter than its diff:
```python
import contextlib

import jax
import jax.numpy as jnp
from jax import lax
from jax.experimental import pallas as pl
from jax.experimental.pallas import tpu as pltpu
from jax.sharding import PartitionSpec as P

F32, BF16 = jnp.float32, jnp.bfloat16
MESH = pl.DeviceIdType.MESH
NT = (((1,), (1,)), ((), ()))
TN = (((0,), (0,)), ((), ()))
VMEM_LIMIT = 61 * 1024 * 1024
SCALE = 32**-0.5
TRACE = False


def scope(name):
    return jax.named_scope(name) if TRACE else contextlib.nullcontext()


def dot(a, b, dims=(((1,), (0,)), ((), ()))):
    return lax.dot_general(a, b, dims, preferred_element_type=F32)


def mod4(v):
    return lax.rem(v + 8, 4)


def gray(k):
    return k + lax.div(k, 2) - 2 * lax.div(k, 3)


def spread_map(rep, out):
    row = lax.broadcasted_iota(jnp.int32, (128, 128), 0)
    for i in range(16):
        out[:, i * 128 : (i + 1) * 128] = jnp.where(lax.rem(row, 16) == i, rep, 0.0).astype(BF16)


def kernel(
    feat, pair_in, adj, wq, wk, wv, wg, bg, wch, wo,
    out, couple,
    pair, qf, ag, kv, bias, dbias, dbin, pbuf, dpbuf, kbuf, vbuf, qbd, dabd, fac, sbuf, pb, dsb, wexp,
    stout, stin, ipart, part, in_x, acc, hopl, in_l, hopy, in_y, zout, zin,
    pin, pout, zs, zr, as_, ar, ys, yr, ls, lr, xs, xr, bs, br, ss, sr, es, er,
    rxs, rxr, rls, rlr, rys, ryr, rzs, rzr,
):
    s, r = lax.axis_index("seq"), lax.axis_index("res")
    zh, c = lax.div(s, 2), lax.rem(s, 2)
    y, x, zl = lax.div(r, 8), lax.rem(lax.div(r, 2), 4), lax.rem(r, 2)
    role = mod4(y - zh)
    jb = x * 2 + zl

    def device(zh_, c_, y_, x_, zl_):
        return (zh_ * 2 + c_, y_ * 8 + x_ * 2 + zl_)

    def to_z(d):
        return device(mod4(zh + d), c, y, x, zl)

    def to_y(d):
        return device(zh, c, mod4(y + d), x, zl)

    def to_x(d):
        return device(zh, c, y, mod4(x + d), zl)

    dev_zl = device(zh, c, y, x, 1 - zl)
    dev_core = device(zh, 1 - c, y, x, zl)

    def remote(src, dst, ssem, rsem, dev):
        return pltpu.make_async_remote_copy(
            src_ref=src, dst_ref=dst, send_sem=ssem, recv_sem=rsem,
            device_id=dev, device_id_type=MESH,
        )

    def pair_copy(g):
        rows = pl.ds(16 * g, 16)
        return pltpu.make_async_copy(pair_in.at[rows], pair.at[rows], pin.at[g])

    def couple_copy(g):
        rows = pl.ds(16 * g, 16)
        return pltpu.make_async_copy(pair.at[rows], couple.at[rows], pout.at[g])

    def seq_of(u):
        return 2 * mod4(zh - gray(lax.div(u, 2))) + lax.rem(u, 2)

    def z_copy(src, dst, ssem, rsem, d, owner):
        return remote(src, dst.at[pl.ds(2 * owner, 2)], ssem.at[d - 1], rsem.at[d - 1], to_z(d))

    def y_copy(u, d):
        src = feat.at[u] if u < 2 else qf.at[seq_of(u)]
        return remote(src, kv.at[seq_of(u), jb], ys.at[u, d - 1], yr.at[u], to_y(d))

    def l_copy(u, b):
        here = kv.at[seq_of(u), b]
        return remote(here, here, ls.at[u], lr.at[u], dev_zl)

    def x_copy(u, d, owner):
        here = kv.at[seq_of(u), pl.ds(2 * owner, 2)]
        return remote(here, here, xs.at[u, d - 1], xr.at[u, d - 1], to_x(d))

    def stage_y(u):
        if u >= 2 and u % 2 == 0:
            d = (0, 1, 3, 2)[u // 2]
            z_copy(feat, qf, zs, zr, d, mod4(zh - d)).wait_recv()

        @pl.when(role == 0)
        def _():
            for d in (1, 3, 2):
                y_copy(u, d).start()
            kv[seq_of(u), jb] = feat[u] if u < 2 else qf[seq_of(u)]

    def stage_l(u):
        @pl.when(role != 0)
        def _():
            remote(
                kv.at[seq_of(u), jb], kv.at[seq_of(u), jb], ys.at[u, 0], yr.at[u], to_y(1)
            ).wait_recv()

        l_copy(u, jb).start()

    def stage_x(u):
        l_copy(u, 2 * x + 1 - zl).wait_recv()
        for d in (1, 3, 2):
            x_copy(u, d, x).start()

    def stage_w(u):
        for d in (1, 3, 2):
            x_copy(u, d, mod4(x - d)).wait_recv()

    for g in range(4):
        pair_copy(g).start()
    qf[pl.ds(2 * zh, 2)] = feat[...]
    ag[pl.ds(2 * zh, 2)] = adj[...]

    with scope("barrier"):
        barrier = pltpu.get_barrier_semaphore()
        partners = [to_z(d) for d in (1, 2, 3)] + [to_y(d) for d in (1, 2, 3)]
        partners += [to_x(d) for d in (1, 2, 3)] + [dev_zl, dev_core]
        for dev in partners:
            pl.semaphore_signal(barrier, inc=1, device_id=dev, device_id_type=MESH)
        pl.semaphore_wait(barrier, len(partners))

    stage_y(0)
    stage_y(1)
    for d in (1, 3, 2):
        z_copy(feat, qf, zs, zr, d, zh).start()
    for d in (1, 3, 2):
        z_copy(adj, ag, as_, ar, d, zh).start()

    row = lax.broadcasted_iota(jnp.int32, (128, 8), 0)
    col = lax.broadcasted_iota(jnp.int32, (128, 8), 1)
    rep = dot(jnp.where(lax.div(row, 16) == col, 1.0, 0.0).astype(BF16), wch[...], NT)
    spread_map(rep, wexp)

    def bias_group(g):
        pair_copy(g).wait()
        total = jnp.zeros((128, 256), F32)
        for p in range(8):
            i = 16 * g + 2 * p
            both = jnp.concatenate([pair[i], pair[i + 1]], axis=1)
            total += dot(wexp[:, p * 256 : (p + 1) * 256], both, NT)
        for h in range(8):
            bias[c, h * 64 + 16 * g : h * 64 + 16 * g + 16, :] = total[h * 16 : h * 16 + 16]

    with scope("bias_a"):
        bias_group(0)
        bias_group(1)
    with scope("hops_a"):
        stage_l(0)
        stage_l(1)
        stage_y(2)
        stage_y(3)
    with scope("bias_b"):
        bias_group(2)
    with scope("hops_b"):
        stage_y(4)
        stage_y(5)
        stage_x(0)
        stage_x(1)
    with scope("bias_c"):
        bias_group(3)
        swap = remote(bias.at[c], bias.at[c], bs, br, dev_core)
        swap.start()
    with scope("hops_c"):
        stage_y(6)
        stage_y(7)
        stage_l(2)
        stage_l(3)
        for d in (1, 3, 2):
            z_copy(adj, ag, as_, ar, d, mod4(zh - d)).wait_recv()

    lanes = lax.broadcasted_iota(jnp.int32, (64, 256), 1)
    masks = [(lanes >= 32 * h) & (lanes < 32 * h + 32) for h in range(8)]

    def query_side(n, carry):
        rows = qf[n]
        q = (dot(rows, wq[...]) * SCALE).astype(BF16).astype(F32)
        gate = jax.nn.sigmoid(dot(rows, wg[...]) + bg[...])
        dg = dot(ag[n], wo[...], NT)
        da = (dg * gate).astype(BF16).astype(F32)
        fac[n] = dg * gate * (1.0 - gate)
        for h in range(8):
            qbd[n, h * 64 : h * 64 + 64, :] = jnp.where(masks[h], q, 0.0).astype(BF16)
            dabd[n, h * 64 : h * 64 + 64, :] = jnp.where(masks[h], da, 0.0).astype(BF16)
        return carry

    with scope("query_a"):
        lax.fori_loop(0, 4, query_side, 0)
    with scope("hops_d"):
        stage_x(2)
        stage_x(3)
        stage_l(4)
        stage_l(5)
    with scope("query_b"):
        lax.fori_loop(4, 8, query_side, 0)
        remote(bias.at[1 - c], bias.at[1 - c], bs, br, dev_core).wait_recv()

    lane = lax.broadcasted_iota(jnp.int32, (64, 128), 1)

    def stat_copy(n, d):
        return remote(stout.at[n], stin.at[n, d - 1], ss.at[n, d - 1], sr.at[n, d - 1], to_z(d))

    def first(u, carry):
        n = seq_of(u)
        with scope("arrive"):
            stage_w(u)
        with scope("first"):
            rows = kv[n].reshape(512, 256)
            kbuf[n] = dot(rows, wk[...]).astype(BF16)
            vbuf[n] = dot(rows, wv[...]).astype(BF16)
            sbuf[...] = dot(qbd[n], kbuf[n], NT)
            dpbuf[n] = dot(dabd[n], vbuf[n], NT)
            tiles = []
            for h in range(8):
                rows = pl.ds(h * 64, 64)
                s0 = sbuf[rows, 0:256] + bias[0, rows, :]
                s1 = sbuf[rows, 256:512] + bias[1, rows, :]
                top = jnp.max(jnp.maximum(s0, s1), axis=1, keepdims=True)
                p0, p1 = jnp.exp(s0 - top), jnp.exp(s1 - top)
                pbuf[n, rows, 0:256] = p0
                pbuf[n, rows, 256:512] = p1
                total = jnp.sum(p0 + p1, axis=1, keepdims=True)
                mixed = jnp.sum(
                    p0 * dpbuf[n, rows, 0:256] + p1 * dpbuf[n, rows, 256:512],
                    axis=1, keepdims=True,
                )
                tiles.append(jnp.where(lane == 0, top, jnp.where(lane == 1, total, mixed)))
            stout[n] = jnp.concatenate(tiles, axis=0).T[0:8]
            for d in (1, 2, 3):
                stat_copy(n, d).start()

        @pl.when(u < 4)
        def _():
            stage_x(u + 4)

        @pl.when(u < 2)
        def _():
            stage_l(u + 6)

        return carry

    lax.fori_loop(0, 8, first, 0)

    def back_seq(u):
        return 2 * mod4(zh - gray(lax.rem(lax.div(u, 2) + 1, 4))) + lax.rem(u, 2)

    def rx_copy(u, d):
        return remote(
            part.at[u, pl.ds(2 * mod4(x + d), 2)], in_x.at[u, d - 1],
            rxs.at[u, d - 1], rxr.at[u, d - 1], to_x(d),
        )

    def rl_copy(u):
        return remote(hopl.at[u], in_l.at[u], rls.at[u], rlr.at[u], dev_zl)

    def ry_copy(u, k):
        return remote(hopy.at[u], in_y.at[u, k - 1], rys.at[u], ryr.at[u, k - 1], to_y(4 - k))

    def rz_copy(u):
        d = gray(lax.rem(lax.div(u, 2) + 1, 4))
        return remote(zout.at[u], zin.at[u], rzs.at[u], rzr.at[u], to_z(4 - d))

    def back_x(u):
        for d in (1, 3, 2):
            rx_copy(u, d).start()

    def back_l(u):
        for d in (1, 3, 2):
            rx_copy(u, d).wait_recv()

        def total(b):
            return (
                (part[u, 2 * x + b].astype(F32) + in_x[u, 0, b].astype(F32))
                + (in_x[u, 1, b].astype(F32) + in_x[u, 2, b].astype(F32))
            )

        acc[u] = total(zl)
        hopl[u] = total(1 - zl).astype(BF16)
        rl_copy(u).start()

    def back_y(u):
        rl_copy(u).wait_recv()
        acc[u] = acc[u] + in_l[u].astype(F32)
        for k in (1, 2, 3):

            @pl.when(role == k)
            def _():
                hopy[u] = acc[u].astype(BF16)
                ry_copy(u, k).start()

    def back_z(u):
        mine = ipart[u]

        @pl.when(role == 0)
        def _():
            for k in (1, 2, 3):
                ry_copy(u, k).wait_recv()
            acc[u] = (mine + acc[u] + in_y[u, 0].astype(F32)) + (
                in_y[u, 1].astype(F32) + in_y[u, 2].astype(F32)
            )

        @pl.when(role != 0)
        def _():
            acc[u] = mine

        @pl.when(u < 6)
        def _():
            zout[u] = acc[u].astype(BF16)
            rz_copy(u).start()

    dbias[...] = jnp.zeros_like(dbias)

    def second(u, carry):
        n = back_seq(u)
        with scope("stats"):
            for d in (1, 2, 3):
                stat_copy(n, d).wait_recv()
            tops = [stout[n, 0:1]] + [stin[n, d, 0:1] for d in range(3)]
            top = jnp.maximum(jnp.maximum(tops[0], tops[1]), jnp.maximum(tops[2], tops[3]))
            own = jnp.exp(tops[0] - top)
            total, mixed = own * stout[n, 1:2], own * stout[n, 2:3]
            for d in range(3):
                weight = jnp.exp(tops[d + 1] - top)
                total += weight * stin[n, d, 1:2]
                mixed += weight * stin[n, d, 2:3]
            down = lax.broadcasted_iota(jnp.int32, (128, 512), 0)
            ab = jnp.where(down == 0, own / total, mixed / total).T
        with scope("second"):
            for h in range(8):
                rows = pl.ds(h * 64, 64)
                a = ab[h * 64 : h * 64 + 64, 0:1]
                delta = ab[h * 64 : h * 64 + 64, 1:2]
                for half in (0, 1):
                    cols = slice(half * 256, half * 256 + 256)
                    probs = pbuf[n, rows, cols] * a
                    pb[rows, cols] = probs.astype(BF16)
                    ds = probs * (dpbuf[n, rows, cols] - delta)
                    dsb[rows, cols] = ds.astype(BF16)
                    dbias[half, rows, :] += ds
            att_all = dot(pb[...], vbuf[n])
            dq_all = dot(dsb[...], kbuf[n])
            att, dq = jnp.zeros((64, 256), F32), jnp.zeros((64, 256), F32)
            for h in range(8):
                att += jnp.where(masks[h], att_all[h * 64 : h * 64 + 64], 0.0)
                dq += jnp.where(masks[h], dq_all[h * 64 : h * 64 + 64], 0.0)
            dq = (dq * SCALE).astype(BF16)
            dgp = (fac[n] * att).astype(BF16)
            ipart[u] = dot(dq, wq[...], NT) + dot(dgp, wg[...], NT)
            dk = dot(qbd[n], dsb[...], TN).T.astype(BF16)
            dv = dot(dabd[n], pb[...], TN).T.astype(BF16)
            part[u] = (
                (dot(dk, wk[...], NT) + dot(dv, wv[...], NT)).astype(BF16).reshape(8, 64, 256)
            )
        with scope("back"):
            back_x(u)

            @pl.when(u >= 3)
            def _():
                back_l(u - 3)

            @pl.when(u >= 5)
            def _():
                back_y(u - 5)

            @pl.when(u >= 7)
            def _():
                back_z(u - 7)

        return carry

    lax.fori_loop(0, 8, second, 0)

    def couple_group(g):
        rows = jnp.concatenate(
            [
                dbias[c, h * 64 + 16 * g : h * 64 + 16 * g + 16, :]
                + dbin[h * 64 + 16 * g : h * 64 + 16 * g + 16, :]
                for h in range(8)
            ],
            axis=0,
        )
        high = rows.astype(BF16)
        low = (rows - high.astype(F32)).astype(BF16)
        both = jnp.concatenate([high, low], axis=0).T
        for p in range(8):
            w = wexp[:, p * 256 : (p + 1) * 256]
            res = dot(both, jnp.concatenate([w, w], axis=0)).astype(BF16)
            pair[16 * g + 2 * p] = res[:, 0:128]
            pair[16 * g + 2 * p + 1] = res[:, 128:256]
        couple_copy(g).start()

    give = remote(dbias.at[1 - c], dbin, es, er, dev_core)
    give.start()
    with scope("tail_a"):
        back_l(5)
        back_y(3)
        back_z(1)
        back_y(4)
        give.wait_recv()
    with scope("couple_a"):
        couple_group(0)
    with scope("tail_b"):
        back_l(6)
        back_z(2)
        back_y(5)
        back_z(3)
    with scope("couple_b"):
        couple_group(1)
    with scope("tail_c"):
        back_l(7)
        back_z(4)
        back_y(6)
        back_z(5)
    with scope("couple_c"):
        couple_group(2)
    with scope("tail_d"):
        back_y(7)
    with scope("couple_d"):
        couple_group(3)
    with scope("tail_e"):
        back_z(6)
        back_z(7)
        for u in range(6):
            rz_copy(u).wait_recv()
        for e in (0, 1):
            out[e] = (
                (acc[6 + e] + zin[e].astype(F32))
                + (zin[2 + e].astype(F32) + zin[4 + e].astype(F32))
            ).astype(BF16)

    with scope("drain"):
        for d in (1, 3, 2):
            z_copy(feat, qf, zs, zr, d, zh).wait_send()
            z_copy(adj, ag, as_, ar, d, zh).wait_send()
        swap.wait_send()
        give.wait_send()

        @pl.when(role == 0)
        def _():
            for u in range(8):
                for d in (1, 3, 2):
                    y_copy(u, d).wait_send()

        @pl.when(role != 0)
        def _():
            for u in range(8):
                ry_copy(u, 1).wait_send()

        def drain(u, carry):
            l_copy(u, jb).wait_send()
            for d in (1, 3, 2):
                x_copy(u, d, x).wait_send()
                stat_copy(u, d).wait_send()
                rx_copy(u, d).wait_send()
            rl_copy(u).wait_send()

            @pl.when(u < 6)
            def _():
                rz_copy(u).wait_send()

            return carry

        lax.fori_loop(0, 8, drain, 0)
        for g in range(4):
            couple_copy(g).wait()


VM = pl.BlockSpec(memory_space=pltpu.VMEM)
HBM = pl.BlockSpec(memory_space=pl.ANY)
DMA = pltpu.SemaphoreType.DMA


def per_device(feat, pair, adj, wq, wk, wv, wg, bg, wch, wo):
    sds, vmem = jax.ShapeDtypeStruct, pltpu.VMEM
    return pl.pallas_call(
        kernel,
        out_shape=(sds((2, 64, 256), BF16), sds((64, 256, 128), BF16)),
        in_specs=[VM, HBM] + [VM] * 8,
        out_specs=(VM, HBM),
        scratch_shapes=[
            vmem((64, 256, 128), BF16),
            vmem((8, 64, 256), BF16),
            vmem((8, 64, 256), BF16),
            vmem((8, 8, 64, 256), BF16),
            vmem((2, 512, 256), F32),
            vmem((2, 512, 256), F32),
            vmem((512, 256), F32),
            vmem((8, 512, 512), F32),
            vmem((8, 512, 512), F32),
            vmem((8, 512, 256), BF16),
            vmem((8, 512, 256), BF16),
            vmem((8, 512, 256), BF16),
            vmem((8, 512, 256), BF16),
            vmem((8, 64, 256), F32),
            vmem((512, 512), F32),
            vmem((512, 512), BF16),
            vmem((512, 512), BF16),
            vmem((128, 2048), BF16),
            vmem((8, 8, 512), F32),
            vmem((8, 3, 8, 512), F32),
            vmem((8, 64, 256), F32),
            vmem((8, 8, 64, 256), BF16),
            vmem((8, 3, 2, 64, 256), BF16),
            vmem((8, 64, 256), F32),
            vmem((8, 64, 256), BF16),
            vmem((8, 64, 256), BF16),
            vmem((8, 64, 256), BF16),
            vmem((8, 3, 64, 256), BF16),
            vmem((6, 64, 256), BF16),
            vmem((6, 64, 256), BF16),
            DMA((4,)), DMA((4,)),
            DMA((3,)), DMA((3,)), DMA((3,)), DMA((3,)),
            DMA((8, 3)), DMA((8,)), DMA((8,)), DMA((8,)), DMA((8, 3)), DMA((8, 3)),
            DMA, DMA, DMA((8, 3)), DMA((8, 3)), DMA, DMA,
            DMA((8, 3)), DMA((8, 3)), DMA((8,)), DMA((8,)), DMA((8,)), DMA((8, 3)),
            DMA((6,)), DMA((6,)),
        ],
        compiler_params=pltpu.CompilerParams(
            collective_id=0, has_side_effects=True, vmem_limit_bytes=VMEM_LIMIT
        ),
        name="fused",
    )(feat, pair, adj, wq, wk, wv, wg, bg.reshape(1, 256), wch, wo)


def solution(mesh):
    in_specs = (
        P("seq", "res", None), P("res", "seq", None), P("seq", "res", None),
        P(), P(), P(), P(), P(), P(), P(),
    )
    out_specs = (P("seq", "res", None), P("res", "seq", None))
    return jax.shard_map(
        per_device, mesh=mesh, in_specs=in_specs, out_specs=out_specs, check_vma=False
    )
```

time: 970 us -> 95 us (0.10); the launches traced: 954 us -> 94 us
  waiting for transfers between devices: 658 us -> 0 us
  local copies, waits for them, and re-layouts: 192 us -> 7.57 us
  Pallas kernels: 0 us -> 85.8 us
  matrix products: 65.3 us -> 0 us
  other arithmetic: 24.1 us -> 0 us
  between operations: 14.7 us -> 0.64 us
    unnamed x5 -> x0, waiting for transfers between devices: 392 us -> none
    all_gather x2 -> x0, waiting for transfers between devices: 208 us -> none  [the longest x1 154 us: per_device(): lax.all_gather(jnp.concatenate([key_part, value_part], 1).reshape(incomin...]
    dynamic_update_slice x4 -> x0, local copies, waits for them, and re-layouts: 171 us -> none  [per_device(): lax.scan(per_homolog, beginning_position, (query_rows, key_rows, value_ro...]
    pallas_call x0 -> x1, Pallas kernels: none -> 85.8 us  [per_device(): pl.pallas_call(kernel, out_shape=(sds((2, 64, 256), BF16), sds((64, 256,...]
    reduce_scatter x1 -> x0, waiting for transfers between devices: 58.3 us -> none  [per_device(): lax.psum_scatter(d_bias_local, 'seq', scatter_dimension=2, tiled=True)]
    dot_general x22 -> x0, matrix products: 53.5 us -> none  [the longest x2 10.7 us: per_homolog(): jnp.einsum('hij,ihd->jhd', probs_b, d_att_heads, preferred_element_type=j...]
    convert_element_type x6 -> x0, other arithmetic: 14.2 us -> none  [the longest x2 14 us: per_homolog(): d_scores_b = d_scores.astype(jnp.bfloat16)]
    sub x2 -> x0, matrix products: 11.8 us -> none  [per_homolog(): probs = jax.nn.softmax(scores, axis=-1)]
  transfers between devices with their start and end apart: 4 -> 0, of which waited for: 4 -> 0; matrix products, arithmetic and copies ran while one was open for 1% -> 0% of each run, Pallas kernels for 0% -> 0%
where the time goes in v2:
time: 95 us; the launch traced here: 94 us
  Pallas kernels  85.8 us (90%)
  local copies, waits for them, and re-layouts  7.57 us (8%)
    pallas_call x1, Pallas kernels, per_device(): pl.pallas_call(kernel, out_shape=(sds((2, 64, 256), BF16), sds((64, 256,...  85.8 us
    unnamed x3, local copies, waits for them, and re-layouts  7.57 us

profile of v2, /device:TPU:4, one launch (start us, length us, event | category | flops | bytes accessed | tf_op | source)
XLA Modules:
  0.0 94.0 jit_solution(387221054769040741)
XLA Ops:
  0.6 1.4 %copy.12.wch = bf16[128,8]{1,0:T(8,128)(2,1)} copy(bf16[128,8]{0,1:T(8,128)(2,1)} %param.18) | data formatting | bytes 4096 | tf_op args[8]
  2.0 85.8 %fused.1 = (bf16[2,64,256]{2,1,0:T(8,128)(2,1)}, bf16[64,256,128]{2,1,0:T(8,128)(2,1)}) custom-call(bf16[2,64,256]{2,1,0:T(8,128)(2,1)} %feat.1, bf16[64,256,128]{2,1,0:T(8,128)(2,1)} %pair_in.1, bf16[2,64,256]{2,1,0:T(8,128)(2,1)} %adj.1, bf16[256,256]{1,0:T(8,128)(2,1)} %wq.1, bf16[256,256]{1,0:T(8,128)(2,1)} %wk.1, bf16[256,256]{1,0:T(8,128)(2,1)} %wv.1, ...), custom_call_target="tpu_custom_call" | custom-call | tf_op jit(solution)/shard_map/fused/pallas_call | solution.py:496
  87.9 1.5 %copy.15 = bf16[2,64,256]{2,1,0:T(8,128)(2,1)} copy(bf16[2,64,256]{2,1,0:T(8,128)(2,1)} %get-tuple-element.4) | data formatting | bytes 131072
  89.3 4.7 %copy.16 = bf16[64,256,128]{2,1,0:T(8,128)(2,1)} copy(bf16[64,256,128]{2,1,0:T(8,128)(2,1)} %get-tuple-element.5) | data formatting | bytes 8388608

commit v3 on v0

v3 whole, which is shorter than its diff:
```python
import jax
import jax.numpy as jnp
from jax import lax
from jax.experimental import pallas as pl
from jax.experimental.pallas import tpu as pltpu
from jax.sharding import PartitionSpec as P

F32, BF16 = jnp.float32, jnp.bfloat16
MESH = pl.DeviceIdType.MESH
NT = (((1,), (1,)), ((), ()))
TN = (((0,), (0,)), ((), ()))
VMEM_LIMIT = 61 * 1024 * 1024
SCALE = 32**-0.5
LAGS = (3, 5)
SHIFT = 8


def dot(a, b, dims=(((1,), (0,)), ((), ()))):
    return lax.dot_general(a, b, dims, preferred_element_type=F32)


def mod4(v):
    return lax.rem(v + 8, 4)


def first_chunk(p, zh):
    later = lax.div(p + 3, 4)
    return (1 - later) * zh + later * (p - 1 + lax.div(p + 3 - zh, 4))


def second_chunk(p, zh):
    last = lax.div(p, 3)
    return last * zh + (1 - last) * (p + lax.div(p + 4 - zh, 4))


def differ(a, b):
    return lax.div((a - b) * (a - b) + 8, 9)


def spread_map(rep, out):
    row = lax.broadcasted_iota(jnp.int32, (128, 128), 0)
    for i in range(16):
        out[:, i * 128 : (i + 1) * 128] = jnp.where(lax.rem(row, 16) == i, rep, 0.0).astype(BF16)


def kernel(
    feat, pair_in, adj, wq_in, wk_in, wv_in, wg_in, bg, wch, wo_in,
    out, db,
    wq, wk, wv, wg, wo, pair, qf, ag, kv, bias, dbias, dbin, pbuf, dpbuf, kbuf, vbuf, qbd, dabd, fac,
    sbuf, pb, dsb, wexp, stout, stin, dbout, ebuf, ipart, part, in_x, hop, in_y, acc, tout, tin, zout, zin,
    win, pin, pout, zs, zr, as_, ar, vs, vr, ys, yr, xs, xr, bs, br, ss, sr, es, er,
    rxs, rxr, rys, ryr, rts, rtr, rzs, rzr,
):
    s, r = lax.axis_index("seq"), lax.axis_index("res")
    zh, c = lax.div(s, 2), lax.rem(s, 2)
    y, x, zl = lax.div(r, 8), lax.rem(lax.div(r, 2), 4), lax.rem(r, 2)
    off_a = differ(y, zh)
    off_b = lax.div(differ(x, y) + differ(y, zh) + 1, 2)

    def wide_at(e):
        return (1 - e) * x + e * y

    def thin_at(e):
        return (1 - e) * y + e * x

    def device(zh_, c_, y_, x_, zl_):
        return (zh_ * 2 + c_, y_ * 8 + x_ * 2 + zl_)

    def to_z(d):
        return device(mod4(zh + d), c, y, x, zl)

    def to_y(d):
        return device(zh, c, mod4(y + d), x, zl)

    def to_x(d):
        return device(zh, c, y, mod4(x + d), zl)

    dev_zl = device(zh, c, y, x, 1 - zl)
    dev_core = device(zh, 1 - c, y, x, zl)

    def remote(src, dst, ssem, rsem, dev):
        return pltpu.make_async_remote_copy(
            src_ref=src, dst_ref=dst, send_sem=ssem, recv_sem=rsem,
            device_id=dev, device_id_type=MESH,
        )

    def pair_copy(g):
        rows = pl.ds(16 * g, 16)
        return pltpu.make_async_copy(pair_in.at[rows], pair.at[rows], pin.at[g])

    def weight_copy(k):
        src, dst = ((wch, None), (wq_in, wq), (wg_in, wg), (wo_in, wo), (wk_in, wk), (wv_in, wv))[k]
        return pltpu.make_async_copy(src, dst, win.at[k - 1])

    def seq_of(u):
        return 2 * first_chunk(lax.div(u, 2), zh) + lax.rem(u, 2)

    def z_copy(src, dst, ssem, rsem, d, owner):
        return remote(src, dst.at[pl.ds(2 * owner, 2)], ssem.at[d - 1], rsem.at[d - 1], to_z(d))

    dev_swapped = device(y, c, zh, x, zl)
    dev_next, dev_previous = device(y, c, x, zh, zl), device(x, c, zh, y, zl)

    def wide_to(e, d):
        xx, yy = (1 - e) * mod4(x + d) + e * x, e * mod4(y + d) + (1 - e) * y
        return device(zh, c, yy, xx, zl)

    def thin_to(e, k, cross):
        return device(zh, c, (1 - e) * k + e * y, e * k + (1 - e) * x, lax.rem(zl + cross, 2))

    def e_copy(e):
        return remote(
            feat.at[e], ebuf.at[e], vs.at[e], vr.at[e], (dev_swapped, dev_next)[e]
        )

    def y_copy(src, e, d, cross):
        k = thin_at(e)
        here = kv.at[2 * k + e, 2 * wide_at(e) + zl]
        return remote(
            src, here, ys.at[e, d, cross], yr.at[2 * k + e, cross], thin_to(e, mod4(k + d), cross)
        )

    Y_ALL = [(d, cross) for d in (1, 3, 2, 0) for cross in (0, 1) if d or cross]

    def stage_y(src, e):
        for d, cross in Y_ALL:
            y_copy(src, e, d, cross).start()
        kv[2 * thin_at(e) + e, 2 * wide_at(e) + zl] = src[...]

    def y_arrived(u):
        n, e = seq_of(u), lax.rem(u, 2)

        def wait(cross, b):
            here = kv.at[n, b]
            remote(here, here, ys.at[0, 0, cross], yr.at[n, cross], dev_zl).wait_recv()

        pl.when(thin_at(e) != first_chunk(lax.div(u, 2), zh))(
            lambda: wait(0, 2 * wide_at(e) + zl)
        )
        wait(1, 2 * wide_at(e) + 1 - zl)

    def x_copy(u, d, owner):
        here = kv.at[seq_of(u), pl.ds(2 * owner, 2)]
        return remote(here, here, xs.at[u, d - 1], xr.at[u, d - 1], wide_to(lax.rem(u, 2), d))

    def stage_x(u):
        for d in (1, 3, 2):
            x_copy(u, d, wide_at(lax.rem(u, 2))).start()

    def stage_w(u):
        for d in (1, 3, 2):
            x_copy(u, d, mod4(wide_at(lax.rem(u, 2)) - d)).wait_recv()

    barrier = pltpu.get_barrier_semaphore()
    partners = [to_z(d) for d in (1, 2, 3)] + [to_y(d) for d in (1, 2, 3)]
    partners += [device(zh, c, mod4(y + d), x, 1 - zl) for d in (0, 1, 2, 3)]
    partners += [device(zh, c, y, mod4(x + d), 1 - zl) for d in (1, 2, 3)]
    partners += [to_x(d) for d in (1, 2, 3)] + [dev_core]
    for dev in partners:
        pl.semaphore_signal(barrier, inc=1, device_id=dev, device_id_type=MESH)

    @pl.when(off_a != 0)
    def _():
        pl.semaphore_signal(barrier, inc=1, device_id=dev_swapped, device_id_type=MESH)

    @pl.when(off_b != 0)
    def _():
        pl.semaphore_signal(barrier, inc=1, device_id=dev_next, device_id_type=MESH)
        pl.semaphore_signal(barrier, inc=1, device_id=dev_previous, device_id_type=MESH)

    for g in range(4):
        pair_copy(g).start()
    for k in range(1, 6):
        weight_copy(k).start()
    qf[pl.ds(2 * zh, 2)] = feat[...]
    ag[pl.ds(2 * zh, 2)] = adj[...]
    row = lax.broadcasted_iota(jnp.int32, (128, 8), 0)
    col = lax.broadcasted_iota(jnp.int32, (128, 8), 1)
    rep = dot(jnp.where(lax.div(row, 16) == col, 1.0, 0.0).astype(BF16), wch[...])
    spread_map(rep, wexp)
    dbias[...] = jnp.zeros_like(dbias)
    pl.semaphore_wait(barrier, len(partners) + off_a + 2 * off_b)

    @pl.when(off_a == 0)
    def _():
        stage_y(feat.at[0], 0)

    @pl.when(off_a != 0)
    def _():
        e_copy(0).start()

    @pl.when(off_b == 0)
    def _():
        stage_y(feat.at[1], 1)

    @pl.when(off_b != 0)
    def _():
        e_copy(1).start()

    for d in (1, 3, 2):
        z_copy(feat, qf, zs, zr, d, zh).start()

    def bias_group(g):
        pair_copy(g).wait()
        total = jnp.zeros((128, 256), F32)
        for p in range(8):
            i = 16 * g + 2 * p
            both = jnp.concatenate([pair[i], pair[i + 1]], axis=1)
            total += dot(wexp[:, p * 256 : (p + 1) * 256], both, NT)
        for h in range(8):
            bias[c, h * 64 + 16 * g : h * 64 + 16 * g + 16, :] = total[h * 16 : h * 16 + 16]

    bias_group(0)
    bias_group(1)
    bias_group(2)
    y_arrived(0)
    stage_x(0)

    @pl.when(off_b != 0)
    def _():
        e_copy(1).wait_recv()
        stage_y(ebuf.at[1], 1)

    @pl.when(off_a != 0)
    def _():
        e_copy(0).wait_recv()
        stage_y(ebuf.at[0], 0)

    for d in (1, 3, 2):
        z_copy(adj, ag, as_, ar, d, zh).start()
    bias_group(3)
    swap = remote(bias.at[c], bias.at[c], bs, br, dev_core)
    swap.start()
    for k in range(1, 6):
        weight_copy(k).wait()

    lanes = lax.broadcasted_iota(jnp.int32, (64, 256), 1)
    masks = [(lanes >= 32 * h) & (lanes < 32 * h + 32) for h in range(8)]

    def query_side(n):
        rows = qf[n]
        q = (dot(rows, wq[...]) * SCALE).astype(BF16).astype(F32)
        gate = jax.nn.sigmoid(dot(rows, wg[...]) + bg[...])
        dg = dot(ag[n], wo[...], NT)
        da = (dg * gate).astype(BF16).astype(F32)
        fac[n] = dg * gate * (1.0 - gate)
        for h in range(8):
            qbd[n, h * 64 : h * 64 + 64, :] = jnp.where(masks[h], q, 0.0).astype(BF16)
            dabd[n, h * 64 : h * 64 + 64, :] = jnp.where(masks[h], da, 0.0).astype(BF16)

    query_side(seq_of(0))
    query_side(seq_of(1))
    y_arrived(1)
    stage_x(1)
    y_arrived(2)
    stage_x(2)
    y_arrived(3)
    stage_x(3)
    remote(bias.at[1 - c], bias.at[1 - c], bs, br, dev_core).wait_recv()

    lane = lax.broadcasted_iota(jnp.int32, (64, 128), 1)

    def stat_copy(n, d):
        return remote(stout.at[n], stin.at[n, d - 1], ss.at[n, d - 1], sr.at[n, d - 1], to_z(d))

    def first(u):
        n = seq_of(u)
        @pl.when((u >= 2) & (lax.rem(u, 2) == 0))
        def _():
            owner = first_chunk(lax.div(u, 2), zh)
            z_copy(feat, qf, zs, zr, mod4(zh - owner), owner).wait_recv()
            z_copy(adj, ag, as_, ar, mod4(zh - owner), owner).wait_recv()

        @pl.when(u >= 2)
        def _():
            query_side(n)

        stage_w(u)
        rows = kv[n].reshape(512, 256)
        kbuf[n] = dot(rows, wk[...]).astype(BF16)
        vbuf[n] = dot(rows, wv[...]).astype(BF16)
        sbuf[...] = dot(qbd[n], kbuf[n], NT)
        dpbuf[n] = dot(dabd[n], vbuf[n], NT)
        tiles = []
        for h in range(8):
            rows = pl.ds(h * 64, 64)
            s0 = sbuf[rows, 0:256] + bias[0, rows, :]
            s1 = sbuf[rows, 256:512] + bias[1, rows, :]
            top = jnp.max(jnp.maximum(s0, s1), axis=1, keepdims=True)
            p0, p1 = jnp.exp(s0 - top), jnp.exp(s1 - top)
            pbuf[n, rows, 0:256] = p0
            pbuf[n, rows, 256:512] = p1
            total = jnp.sum(p0 + p1, axis=1, keepdims=True)
            mixed = jnp.sum(
                p0 * dpbuf[n, rows, 0:256] + p1 * dpbuf[n, rows, 256:512], axis=1, keepdims=True
            )
            tiles.append(jnp.where(lane == 0, top, jnp.where(lane == 1, total, mixed)))
        stats = jnp.concatenate(tiles, axis=0).T[0:4]
        for k in range(4):
            stout[n, 4 * k : 4 * k + 4, :] = stats[:, 128 * k : 128 * k + 128]
        for d in (1, 3, 2):
            stat_copy(n, d).start()

        @pl.when(u < 4)
        def _():
            y_arrived(u + 4)
            stage_x(u + 4)

    def odd(u):
        return 1 - lax.rem(u, 2)

    def back_seq(u):
        return 2 * second_chunk(lax.div(u, 2), zh) + odd(u)

    def rx_copy(u, d):
        e = odd(u)
        return remote(
            part.at[u, pl.ds(2 * mod4(wide_at(e) + d), 2)], in_x.at[u, d - 1],
            rxs.at[u, d - 1], rxr.at[u, d - 1], wide_to(e, d),
        )

    def ry_copy(u, cross):
        e, k = odd(u), second_chunk(lax.div(u, 2), zh)
        slot = 2 * mod4(thin_at(e) - k) + cross
        return remote(
            hop.at[u, cross], in_y.at[e, slot], rys.at[u, cross], ryr.at[e, slot],
            thin_to(e, k, cross),
        )

    def ry_arrived(e, slot):
        remote(hop.at[0, 0], in_y.at[e, slot], rys.at[0, 0], ryr.at[e, slot], dev_zl).wait_recv()

    def rt_copy(e):
        return remote(
            tout.at[e], tin.at[e], rts.at[e], rtr.at[e], (dev_swapped, dev_previous)[e]
        )

    def rz_copy(u):
        owner = second_chunk(lax.div(u, 2), zh)
        slot = 2 * (mod4(owner - zh) - 1) + odd(u)
        return remote(
            zout.at[u], zin.at[slot], rzs.at[u], rzr.at[slot], device(owner, c, y, x, zl)
        )

    def rz_arrived(slot):
        remote(zout.at[slot], zin.at[slot], rzs.at[slot], rzr.at[slot], to_z(1)).wait_recv()

    def back_x(u):
        for d in (1, 3, 2):
            rx_copy(u, d).start()

    def x_total(u, b):
        mine = part[u, 2 * wide_at(odd(u)) + b]
        return (mine.astype(F32) + in_x[u, 0, b].astype(F32)) + (
            in_x[u, 1, b].astype(F32) + in_x[u, 2, b].astype(F32)
        )

    def back_y(u):
        for d in (1, 3, 2):
            rx_copy(u, d).wait_recv()
        hop[u, 1] = x_total(u, 1 - zl).astype(BF16)
        ry_copy(u, 1).start()
        own = x_total(u, zl)
        away = thin_at(odd(u)) != second_chunk(lax.div(u, 2), zh)

        @pl.when(away)
        def _():
            hop[u, 0] = own.astype(BF16)
            ry_copy(u, 0).start()

        @pl.when(jnp.logical_not(away))
        def _():
            acc[odd(u)] = own

    def back_t(u):
        def finish(e):
            for slot in range(1, 8):
                ry_arrived(e, slot)
            got = [in_y[e, slot].astype(F32) for slot in range(1, 8)]
            total = ((acc[e] + got[0]) + (got[1] + got[2])) + ((got[3] + got[4]) + (got[5] + got[6]))
            acc[e] = total

            @pl.when((off_a, off_b)[e] != 0)
            def _():
                tout[e] = total.astype(BF16)
                rt_copy(e).start()

        k = second_chunk(lax.div(u, 2), zh)
        for e in (0, 1):
            pl.when((odd(u) == e) & (thin_at(e) == k))(lambda: finish(e))

    def second(u):
        n = back_seq(u)
        for d in (1, 3, 2):
            stat_copy(n, d).wait_recv()

        def wide(v):
            return jnp.concatenate([v[4 * k : 4 * k + 4] for k in range(4)], axis=1)

        own_stats = wide(stout[n])
        others = [wide(stin[n, d]) for d in range(3)]
        tops = [own_stats[0:1]] + [o[0:1] for o in others]
        top = jnp.maximum(jnp.maximum(tops[0], tops[1]), jnp.maximum(tops[2], tops[3]))
        own = jnp.exp(tops[0] - top)
        total, mixed = own * own_stats[1:2], own * own_stats[2:3]
        for d in range(3):
            weight = jnp.exp(tops[d + 1] - top)
            total += weight * others[d][1:2]
            mixed += weight * others[d][2:3]
        down = lax.broadcasted_iota(jnp.int32, (128, 512), 0)
        ab = jnp.where(down == 0, own / total, mixed / total).T
        for h in range(8):
            rows = pl.ds(h * 64, 64)
            a = ab[h * 64 : h * 64 + 64, 0:1]
            delta = ab[h * 64 : h * 64 + 64, 1:2]
            for half in (0, 1):
                cols = slice(half * 256, half * 256 + 256)
                probs = pbuf[n, rows, cols] * a
                pb[rows, cols] = probs.astype(BF16)
                ds = probs * (dpbuf[n, rows, cols] - delta)
                dsb[rows, cols] = ds.astype(BF16)
                dbias[half, rows, :] += ds
        att_all = dot(pb[...], vbuf[n])
        dq_all = dot(dsb[...], kbuf[n])
        att, dq = jnp.zeros((64, 256), F32), jnp.zeros((64, 256), F32)
        for h in range(8):
            att += jnp.where(masks[h], att_all[h * 64 : h * 64 + 64], 0.0)
            dq += jnp.where(masks[h], dq_all[h * 64 : h * 64 + 64], 0.0)
        dq = (dq * SCALE).astype(BF16)
        dgp = (fac[n] * att).astype(BF16)
        ipart[u] = dot(dq, wq[...], NT) + dot(dgp, wg[...], NT)

        @pl.when(u < 6)
        def _():
            zout[u] = ipart[u].astype(BF16)
            rz_copy(u).start()

        dk = dot(qbd[n], dsb[...], TN).T.astype(BF16)
        dv = dot(dabd[n], pb[...], TN).T.astype(BF16)
        part[u] = (
            (dot(dk, wk[...], NT) + dot(dv, wv[...], NT)).astype(BF16).reshape(8, 64, 256)
        )
        back_x(u)

    LY, LT = LAGS

    def step(t, carry):
        @pl.when(t < 8)
        def _():
            first(t)

        @pl.when(t >= SHIFT)
        def _():
            second(t - SHIFT)

        for lag, stage in ((LY, back_y), (LT, back_t)):
            if lag < 8:
                pl.when(t >= SHIFT + lag)(lambda: stage(t - SHIFT - lag))

        return carry

    lax.fori_loop(0, 8 + SHIFT, step, 0)
    give = remote(dbias.at[1 - c], dbin, es, er, dev_core)
    give.start()
    waits = [(back_y, u, u + LY) for u in range(8)] + [(back_t, u, u + LT) for u in range(8)]
    for fun, u, when in sorted((w for w in waits if w[2] > 7), key=lambda w: w[2]):
        fun(u)
    give.wait_recv()
    dbout[...] = dbias[c] + dbin[...]
    db_copy = pltpu.make_async_copy(dbout, db, pout)
    db_copy.start()
    for u in range(6):
        rz_arrived(u)

    for e in (0, 1):

        @pl.when((off_a, off_b)[e] != 0)
        def _():
            rt_copy(e).wait_recv()
            acc[e] = tin[e].astype(F32)

    for e in (0, 1):
        out[e] = (
            (acc[e] + ipart[7 - e] + zin[e].astype(F32))
            + (zin[2 + e].astype(F32) + zin[4 + e].astype(F32))
        ).astype(BF16)

    for d in (1, 3, 2):
        z_copy(feat, qf, zs, zr, d, zh).wait_send()
        z_copy(adj, ag, as_, ar, d, zh).wait_send()
    swap.wait_send()
    give.wait_send()

    for e in (0, 1):
        for d, cross in Y_ALL:
            y_copy(feat.at[e], e, d, cross).wait_send()

        @pl.when((off_a, off_b)[e] != 0)
        def _():
            e_copy(e).wait_send()
            rt_copy(e).wait_send()

    def drain(u, carry):
        for d in (1, 3, 2):
            x_copy(u, d, wide_at(lax.rem(u, 2))).wait_send()
            stat_copy(u, d).wait_send()
            rx_copy(u, d).wait_send()
        ry_copy(u, 1).wait_send()

        @pl.when(thin_at(odd(u)) != second_chunk(lax.div(u, 2), zh))
        def _():
            ry_copy(u, 0).wait_send()

        @pl.when(u < 6)
        def _():
            rz_copy(u).wait_send()

        return carry

    lax.fori_loop(0, 8, drain, 0)
    db_copy.wait()


def couple_kernel(db, wch, hom, couple, out, wide, store, sems):
    row = lax.broadcasted_iota(jnp.int32, (128, 8), 0)
    col = lax.broadcasted_iota(jnp.int32, (128, 8), 1)
    rep = dot(jnp.where(lax.div(row, 16) == col, 1.0, 0.0).astype(BF16), wch[...])
    spread_map(rep, wide)
    out[...] = hom[...]

    def copy(g):
        rows = pl.ds(16 * g, 16)
        return pltpu.make_async_copy(store.at[rows], couple.at[rows], sems.at[g])

    for g in range(4):
        rows = jnp.concatenate(
            [db[h * 64 + 16 * g : h * 64 + 16 * g + 16, :] for h in range(8)], axis=0
        )
        high = rows.astype(BF16)
        low = (rows - high.astype(F32)).astype(BF16)
        both = jnp.concatenate([high, low], axis=0).T
        for p in range(8):
            w = wide[:, p * 256 : (p + 1) * 256]
            res = dot(both, jnp.concatenate([w, w], axis=0)).astype(BF16)
            store[16 * g + 2 * p] = res[:, 0:128]
            store[16 * g + 2 * p + 1] = res[:, 128:256]
        copy(g).start()
    for g in range(4):
        copy(g).wait()


VM = pl.BlockSpec(memory_space=pltpu.VMEM)
HBM = pl.BlockSpec(memory_space=pl.ANY)
DMA = pltpu.SemaphoreType.DMA


def per_device(feat, pair, adj, wq, wk, wv, wg, bg, wch, wo):
    sds, vmem = jax.ShapeDtypeStruct, pltpu.VMEM
    wch = wch.T
    hom, db = pl.pallas_call(
        kernel,
        out_shape=(sds((2, 64, 256), BF16), sds((512, 256), F32)),
        in_specs=[VM, HBM, VM, HBM, HBM, HBM, HBM, VM, VM, HBM],
        out_specs=(VM, HBM),
        scratch_shapes=[vmem((256, 256), BF16)] * 5
        + [
            vmem((64, 256, 128), BF16),
            vmem((8, 64, 256), BF16),
            vmem((8, 64, 256), BF16),
            vmem((8, 8, 64, 256), BF16),
            vmem((2, 512, 256), F32),
            vmem((2, 512, 256), F32),
            vmem((512, 256), F32),
            vmem((8, 512, 512), F32),
            vmem((8, 512, 512), F32),
            vmem((8, 512, 256), BF16),
            vmem((8, 512, 256), BF16),
            vmem((8, 512, 256), BF16),
            vmem((8, 512, 256), BF16),
            vmem((8, 64, 256), F32),
            vmem((512, 512), F32),
            vmem((512, 512), BF16),
            vmem((512, 512), BF16),
            vmem((128, 2048), BF16),
            vmem((8, 16, 128), F32),
            vmem((8, 3, 16, 128), F32),
            vmem((512, 256), F32),
            vmem((2, 64, 256), BF16),
            vmem((8, 64, 256), F32),
            vmem((8, 8, 64, 256), BF16),
            vmem((8, 3, 2, 64, 256), BF16),
            vmem((8, 2, 64, 256), BF16),
            vmem((2, 8, 64, 256), BF16),
            vmem((2, 64, 256), F32),
            vmem((2, 64, 256), BF16),
            vmem((2, 64, 256), BF16),
            vmem((6, 64, 256), BF16),
            vmem((6, 64, 256), BF16),
            DMA((5,)), DMA((4,)), DMA,
            DMA((3,)), DMA((3,)), DMA((3,)), DMA((3,)),
            DMA((2,)), DMA((2,)), DMA((2, 4, 2)), DMA((8, 2)), DMA((8, 3)), DMA((8, 3)),
            DMA, DMA, DMA((8, 3)), DMA((8, 3)), DMA, DMA,
            DMA((8, 3)), DMA((8, 3)), DMA((8, 2)), DMA((2, 8)), DMA((2,)), DMA((2,)),
            DMA((6,)), DMA((6,)),
        ],
        compiler_params=pltpu.CompilerParams(
            collective_id=0, has_side_effects=True, vmem_limit_bytes=VMEM_LIMIT
        ),
        name="fused",
    )(feat, pair, adj, wq, wk, wv, wg, bg.reshape(1, 256), wch, wo)
    couple, homolog = pl.pallas_call(
        couple_kernel,
        out_shape=(sds((64, 256, 128), BF16), sds((2, 64, 256), BF16)),
        in_specs=[VM] * 3,
        out_specs=(HBM, VM),
        scratch_shapes=[vmem((128, 2048), BF16), vmem((64, 256, 128), BF16), DMA((4,))],
        compiler_params=pltpu.CompilerParams(vmem_limit_bytes=VMEM_LIMIT),
        name="couple",
    )(db, wch, hom)
    return homolog, couple


def solution(mesh):
    in_specs = (
        P("seq", "res", None), P("res", "seq", None), P("seq", "res", None),
        P(), P(), P(), P(), P(), P(), P(),
    )
    out_specs = (P("seq", "res", None), P("res", "seq", None))
    return jax.shard_map(
        per_device, mesh=mesh, in_specs=in_specs, out_specs=out_specs, check_vma=False
    )
```

time: 970 us -> 82 us (0.08); the launches traced: 954 us -> 81.4 us
  waiting for transfers between devices: 658 us -> 0 us
  local copies, waits for them, and re-layouts: 192 us -> 0 us
  Pallas kernels: 0 us -> 80.8 us
  matrix products: 65.3 us -> 0 us
  other arithmetic: 24.1 us -> 0 us
  between operations: 14.7 us -> 0.64 us
    unnamed x5 -> x0, waiting for transfers between devices: 392 us -> none
    all_gather x2 -> x0, waiting for transfers between devices: 208 us -> none  [the longest x1 154 us: per_device(): lax.all_gather(jnp.concatenate([key_part, value_part], 1).reshape(incomin...]
    dynamic_update_slice x4 -> x0, local copies, waits for them, and re-layouts: 171 us -> none  [per_device(): lax.scan(per_homolog, beginning_position, (query_rows, key_rows, value_ro...]
    pallas_call x0 -> x2, Pallas kernels: none -> 80.8 us  [the longest x1 76.4 us: per_device(): pl.pallas_call(kernel, out_shape=(sds((2, 64, 256), BF16), sds((512, 256)...]
    reduce_scatter x1 -> x0, waiting for transfers between devices: 58.3 us -> none  [per_device(): lax.psum_scatter(d_bias_local, 'seq', scatter_dimension=2, tiled=True)]
    dot_general x22 -> x0, matrix products: 53.5 us -> none  [the longest x2 10.7 us: per_homolog(): jnp.einsum('hij,ihd->jhd', probs_b, d_att_heads, preferred_element_type=j...]
    convert_element_type x6 -> x0, other arithmetic: 14.2 us -> none  [the longest x2 14 us: per_homolog(): d_scores_b = d_scores.astype(jnp.bfloat16)]
    sub x2 -> x0, matrix products: 11.8 us -> none  [per_homolog(): probs = jax.nn.softmax(scores, axis=-1)]
  transfers between devices with their start and end apart: 4 -> 0, of which waited for: 4 -> 0; matrix products, arithmetic and copies ran while one was open for 1% -> 0% of each run, Pallas kernels for 0% -> 0%
where the time goes in v3:
time: 82 us; the launch traced here: 81.4 us
  Pallas kernels  80.8 us (99%)
    pallas_call x1, Pallas kernels, per_device(): pl.pallas_call(kernel, out_shape=(sds((2, 64, 256), BF16), sds((512, 256)...  76.4 us
    pallas_call x1, Pallas kernels, per_device(): pl.pallas_call(couple_kernel, out_shape=(sds((64, 256, 128), BF16), sds((...  4.33 us

profile of v3, /device:TPU:4, one launch (start us, length us, event | category | flops | bytes accessed | tf_op | source)
XLA Modules:
  0.0 81.4 jit_solution(17763550510523949903)
XLA Ops:
  0.6 76.4 %fused.1 = (bf16[2,64,256]{2,1,0:T(8,128)(2,1)}, f32[512,256]{1,0:T(8,128)}) custom-call(bf16[2,64,256]{2,1,0:T(8,128)(2,1)} %feat.1, bf16[64,256,128]{2,1,0:T(8,128)(2,1)} %pair_in.1, bf16[2,64,256]{2,1,0:T(8,128)(2,1)} %adj.1, bf16[256,256]{1,0:T(8,128)(2,1)} %wq_in.1, bf16[256,256]{1,0:T(8,128)(2,1)} %wk_in.1, bf16[256,256]{1,0:T(8,128)(2,1)} %wv_in.1, ...), custom_call_target="tpu_custom_call" | custom-call | tf_op jit(solution)/shard_map/fused/pallas_call | solution.py:560
  77.1 4.3 %couple.1 = (bf16[64,256,128]{2,1,0:T(8,128)(2,1)}, bf16[2,64,256]{2,1,0:T(8,128)(2,1)}) custom-call(f32[512,256]{1,0:T(8,128)} %get-tuple-element.6.db, bf16[8,128]{1,0:T(8,128)(2,1)} %bitcast.3, bf16[2,64,256]{2,1,0:T(8,128)(2,1)} %get-tuple-element.7.hom), custom_call_target="tpu_custom_call" | custom-call | tf_op jit(solution)/shard_map/couple/pallas_call | solution.py:611

commit v4 on v3

--- a/solution.py
+++ b/solution.py
@@ -47,7 +47,7 @@
     feat, pair_in, adj, wq_in, wk_in, wv_in, wg_in, bg, wch, wo_in,
     out, db,
     wq, wk, wv, wg, wo, pair, qf, ag, kv, bias, dbias, dbin, pbuf, dpbuf, kbuf, vbuf, qbd, dabd, fac,
-    sbuf, pb, dsb, wexp, stout, stin, dbout, ebuf, ipart, part, in_x, hop, in_y, acc, tout, tin, zout, zin,
+    sbuf, cw, sp, wexp, stout, stin, dbout, ebuf, ipart, part, in_x, hop, in_y, acc, tout, tin, zout, zin,
     win, pin, pout, zs, zr, as_, ar, vs, vr, ys, yr, xs, xr, bs, br, ss, sr, es, er,
     rxs, rxr, rys, ryr, rts, rtr, rzs, rzr,
 ):
@@ -247,6 +247,8 @@
         for h in range(8):
             qbd[n, h * 64 : h * 64 + 64, :] = jnp.where(masks[h], q, 0.0).astype(BF16)
             dabd[n, h * 64 : h * 64 + 64, :] = jnp.where(masks[h], da, 0.0).astype(BF16)
+        cw[n, :, 0:512] = dot(qbd[n], wk[...], NT).astype(BF16).T
+        cw[n, :, 512:1024] = dot(dabd[n], wv[...], NT).astype(BF16).T
 
     query_side(seq_of(0))
     query_side(seq_of(1))
@@ -416,12 +418,15 @@
             for half in (0, 1):
                 cols = slice(half * 256, half * 256 + 256)
                 probs = pbuf[n, rows, cols] * a
-                pb[rows, cols] = probs.astype(BF16)
+                sp[pl.ds(512 + h * 64, 64), cols] = probs.astype(BF16)
                 ds = probs * (dpbuf[n, rows, cols] - delta)
-                dsb[rows, cols] = ds.astype(BF16)
+                sp[rows, cols] = ds.astype(BF16)
                 dbias[half, rows, :] += ds
-        att_all = dot(pb[...], vbuf[n])
-        dq_all = dot(dsb[...], kbuf[n])
+        both = dot(cw[n], sp[...]).astype(BF16).T
+        part[u] = both.reshape(8, 64, 256)
+        back_x(u)
+        att_all = dot(sp[512:1024, :], vbuf[n])
+        dq_all = dot(sp[0:512, :], kbuf[n])
         att, dq = jnp.zeros((64, 256), F32), jnp.zeros((64, 256), F32)
         for h in range(8):
             att += jnp.where(masks[h], att_all[h * 64 : h * 64 + 64], 0.0)
@@ -434,13 +439,6 @@
         def _():
             zout[u] = ipart[u].astype(BF16)
             rz_copy(u).start()
-
-        dk = dot(qbd[n], dsb[...], TN).T.astype(BF16)
-        dv = dot(dabd[n], pb[...], TN).T.astype(BF16)
-        part[u] = (
-            (dot(dk, wk[...], NT) + dot(dv, wv[...], NT)).astype(BF16).reshape(8, 64, 256)
-        )
-        back_x(u)
 
     LY, LT = LAGS
 
@@ -529,7 +527,7 @@
     out[...] = hom[...]
 
     def copy(g):
-        rows = pl.ds(16 * g, 16)
+        rows = pl.ds(8 * g, 8)
         return pltpu.make_async_copy(store.at[rows], couple.at[rows], sems.at[g])
 
     for g in range(4):
@@ -544,8 +542,9 @@
             res = dot(both, jnp.concatenate([w, w], axis=0)).astype(BF16)
             store[16 * g + 2 * p] = res[:, 0:128]
             store[16 * g + 2 * p + 1] = res[:, 128:256]
-        copy(g).start()
-    for g in range(4):
+            if p % 4 == 3:
+                copy(2 * g + p // 4).start()
+    for g in range(8):
         copy(g).wait()
 
 
@@ -579,8 +578,8 @@
             vmem((8, 512, 256), BF16),
             vmem((8, 64, 256), F32),
             vmem((512, 512), F32),
-            vmem((512, 512), BF16),
-            vmem((512, 512), BF16),
+            vmem((8, 256, 1024), BF16),
+            vmem((1024, 512), BF16),
             vmem((128, 2048), BF16),
             vmem((8, 16, 128), F32),
             vmem((8, 3, 16, 128), F32),
@@ -613,7 +612,7 @@
         out_shape=(sds((64, 256, 128), BF16), sds((2, 64, 256), BF16)),
         in_specs=[VM] * 3,
         out_specs=(HBM, VM),
-        scratch_shapes=[vmem((128, 2048), BF16), vmem((64, 256, 128), BF16), DMA((4,))],
+        scratch_shapes=[vmem((128, 2048), BF16), vmem((64, 256, 128), BF16), DMA((8,))],
         compiler_params=pltpu.CompilerParams(vmem_limit_bytes=VMEM_LIMIT),
         name="couple",
     )(db, wch, hom)

time: 82 us -> 80.3 us (0.979)
  Pallas kernels: 80.8 us -> 79.5 us
    pallas_call x1, Pallas kernels: 76.4 us -> 75.2 us  [per_device(): pl.pallas_call(kernel, out_shape=(sds((2, 64, 256), BF16), sds((512, 256)...]
where the time goes in v4:
time: 80.3 us; the launch traced here: 80.1 us
  Pallas kernels  79.5 us (99%)
    pallas_call x1, Pallas kernels, per_device(): pl.pallas_call(kernel, out_shape=(sds((2, 64, 256), BF16), sds((512, 256)...  75.2 us
    pallas_call x1, Pallas kernels, per_device(): pl.pallas_call(couple_kernel, out_shape=(sds((64, 256, 128), BF16), sds((...  4.23 us

profile of v4, /device:TPU:4, one launch (start us, length us, event | category | flops | bytes accessed | tf_op | source)
XLA Modules:
  0.0 80.1 jit_solution(16136179950768780025)
XLA Ops:
  0.6 75.2 %fused.1 = (bf16[2,64,256]{2,1,0:T(8,128)(2,1)}, f32[512,256]{1,0:T(8,128)}) custom-call(bf16[2,64,256]{2,1,0:T(8,128)(2,1)} %feat.1, bf16[64,256,128]{2,1,0:T(8,128)(2,1)} %pair_in.1, bf16[2,64,256]{2,1,0:T(8,128)(2,1)} %adj.1, bf16[256,256]{1,0:T(8,128)(2,1)} %wq_in.1, bf16[256,256]{1,0:T(8,128)(2,1)} %wk_in.1, bf16[256,256]{1,0:T(8,128)(2,1)} %wv_in.1, ...), custom_call_target="tpu_custom_call" | custom-call | tf_op jit(solution)/shard_map/fused/pallas_call | solution.py:559
  75.9 4.2 %couple.1 = (bf16[64,256,128]{2,1,0:T(8,128)(2,1)}, bf16[2,64,256]{2,1,0:T(8,128)(2,1)}) custom-call(f32[512,256]{1,0:T(8,128)} %get-tuple-element.6.db, bf16[8,128]{1,0:T(8,128)(2,1)} %bitcast.3, bf16[2,64,256]{2,1,0:T(8,128)(2,1)} %get-tuple-element.7.hom), custom_call_target="tpu_custom_call" | custom-call | tf_op jit(solution)/shard_map/couple/pallas_call | solution.py:610

commit v5 on v4

--- a/solution.py
+++ b/solution.py
@@ -44,9 +44,9 @@
 
 
 def kernel(
-    feat, pair_in, adj, wq_in, wk_in, wv_in, wg_in, bg, wch, wo_in,
+    feat_in, pair_in, adj_in, wq_in, wk_in, wv_in, wg_in, bg_in, wch_in, wo_in,
     out, db,
-    wq, wk, wv, wg, wo, pair, qf, ag, kv, bias, dbias, dbin, pbuf, dpbuf, kbuf, vbuf, qbd, dabd, fac,
+    feat, bg, wch, wq, wk, wv, wg, wo, pair, qf, ag, kv, bias, dbias, dbin, pbuf, dpbuf, kbuf, vbuf, qbd, dabd, fac,
     sbuf, cw, sp, wexp, stout, stin, dbout, ebuf, ipart, part, in_x, hop, in_y, acc, tout, tin, zout, zin,
     win, pin, pout, zs, zr, as_, ar, vs, vr, ys, yr, xs, xr, bs, br, ss, sr, es, er,
     rxs, rxr, rys, ryr, rts, rtr, rzs, rzr,
@@ -89,8 +89,11 @@
         return pltpu.make_async_copy(pair_in.at[rows], pair.at[rows], pin.at[g])
 
     def weight_copy(k):
-        src, dst = ((wch, None), (wq_in, wq), (wg_in, wg), (wo_in, wo), (wk_in, wk), (wv_in, wv))[k]
-        return pltpu.make_async_copy(src, dst, win.at[k - 1])
+        src, dst = (
+            (feat_in, feat), (wch_in, wch), (adj_in, ag.at[pl.ds(2 * zh, 2)]), (bg_in, bg),
+            (wq_in, wq), (wg_in, wg), (wo_in, wo), (wk_in, wk), (wv_in, wv),
+        )[k]
+        return pltpu.make_async_copy(src, dst, win.at[k])
 
     def seq_of(u):
         return 2 * first_chunk(lax.div(u, 2), zh) + lax.rem(u, 2)
@@ -144,7 +147,7 @@
         return remote(here, here, xs.at[u, d - 1], xr.at[u, d - 1], wide_to(lax.rem(u, 2), d))
 
     def stage_x(u):
-        for d in (1, 3, 2):
+        for d in (2, 1, 3):
             x_copy(u, d, wide_at(lax.rem(u, 2))).start()
 
     def stage_w(u):
@@ -168,12 +171,15 @@
         pl.semaphore_signal(barrier, inc=1, device_id=dev_next, device_id_type=MESH)
         pl.semaphore_signal(barrier, inc=1, device_id=dev_previous, device_id_type=MESH)
 
+    for k in range(4):
+        weight_copy(k).start()
     for g in range(4):
         pair_copy(g).start()
-    for k in range(1, 6):
+    for k in range(4, 9):
         weight_copy(k).start()
+    weight_copy(0).wait()
+    weight_copy(1).wait()
     qf[pl.ds(2 * zh, 2)] = feat[...]
-    ag[pl.ds(2 * zh, 2)] = adj[...]
     row = lax.broadcasted_iota(jnp.int32, (128, 8), 0)
     col = lax.broadcasted_iota(jnp.int32, (128, 8), 1)
     rep = dot(jnp.where(lax.div(row, 16) == col, 1.0, 0.0).astype(BF16), wch[...])
@@ -226,12 +232,13 @@
         e_copy(0).wait_recv()
         stage_y(ebuf.at[0], 0)
 
+    weight_copy(2).wait()
     for d in (1, 3, 2):
-        z_copy(adj, ag, as_, ar, d, zh).start()
+        z_copy(ag.at[pl.ds(2 * zh, 2)], ag, as_, ar, d, zh).start()
     bias_group(3)
     swap = remote(bias.at[c], bias.at[c], bs, br, dev_core)
     swap.start()
-    for k in range(1, 6):
+    for k in range(3, 9):
         weight_copy(k).wait()
 
     lanes = lax.broadcasted_iota(jnp.int32, (64, 256), 1)
@@ -271,7 +278,7 @@
         def _():
             owner = first_chunk(lax.div(u, 2), zh)
             z_copy(feat, qf, zs, zr, mod4(zh - owner), owner).wait_recv()
-            z_copy(adj, ag, as_, ar, mod4(zh - owner), owner).wait_recv()
+            z_copy(ag.at[pl.ds(2 * zh, 2)], ag, as_, ar, mod4(zh - owner), owner).wait_recv()
 
         @pl.when(u >= 2)
         def _():
@@ -348,7 +355,7 @@
         remote(zout.at[slot], zin.at[slot], rzs.at[slot], rzr.at[slot], to_z(1)).wait_recv()
 
     def back_x(u):
-        for d in (1, 3, 2):
+        for d in (2, 1, 3):
             rx_copy(u, d).start()
 
     def x_total(u, b):
@@ -485,7 +492,7 @@
 
     for d in (1, 3, 2):
         z_copy(feat, qf, zs, zr, d, zh).wait_send()
-        z_copy(adj, ag, as_, ar, d, zh).wait_send()
+        z_copy(ag.at[pl.ds(2 * zh, 2)], ag, as_, ar, d, zh).wait_send()
     swap.wait_send()
     give.wait_send()
 
@@ -559,9 +566,10 @@
     hom, db = pl.pallas_call(
         kernel,
         out_shape=(sds((2, 64, 256), BF16), sds((512, 256), F32)),
-        in_specs=[VM, HBM, VM, HBM, HBM, HBM, HBM, VM, VM, HBM],
+        in_specs=[HBM] * 10,
         out_specs=(VM, HBM),
-        scratch_shapes=[vmem((256, 256), BF16)] * 5
+        scratch_shapes=[vmem((2, 64, 256), BF16), vmem((1, 256), F32), vmem((8, 128), BF16)]
+        + [vmem((256, 256), BF16)] * 5
         + [
             vmem((64, 256, 128), BF16),
             vmem((8, 64, 256), BF16),
@@ -595,7 +603,7 @@
             vmem((2, 64, 256), BF16),
             vmem((6, 64, 256), BF16),
             vmem((6, 64, 256), BF16),
-            DMA((5,)), DMA((4,)), DMA,
+            DMA((9,)), DMA((4,)), DMA,
             DMA((3,)), DMA((3,)), DMA((3,)), DMA((3,)),
             DMA((2,)), DMA((2,)), DMA((2, 4, 2)), DMA((8, 2)), DMA((8, 3)), DMA((8, 3)),
             DMA, DMA, DMA((8, 3)), DMA((8, 3)), DMA, DMA,

time: 80.3 us -> 79.6 us (level)
  no operation moved by 1% of the time
where the time goes in v5:
time: 79.6 us; the launch traced here: 79.5 us
  Pallas kernels  78.9 us (99%)
    pallas_call x1, Pallas kernels, per_device(): pl.pallas_call(kernel, out_shape=(sds((2, 64, 256), BF16), sds((512, 256)...  74.6 us
    pallas_call x1, Pallas kernels, per_device(): pl.pallas_call(couple_kernel, out_shape=(sds((64, 256, 128), BF16), sds((...  4.23 us

profile of v5, /device:TPU:4, one launch (start us, length us, event | category | flops | bytes accessed | tf_op | source)
XLA Modules:
  0.0 79.5 jit_solution(4863420833545395236)
XLA Ops:
  0.6 74.6 %fused.1 = (bf16[2,64,256]{2,1,0:T(8,128)(2,1)}, f32[512,256]{1,0:T(8,128)}) custom-call(bf16[2,64,256]{2,1,0:T(8,128)(2,1)} %feat_in.1, bf16[64,256,128]{2,1,0:T(8,128)(2,1)} %pair_in.1, bf16[2,64,256]{2,1,0:T(8,128)(2,1)} %adj_in.1, bf16[256,256]{1,0:T(8,128)(2,1)} %wq_in.1, bf16[256,256]{1,0:T(8,128)(2,1)} %wk_in.1, bf16[256,256]{1,0:T(8,128)(2,1)} %wv_in.1, ...), custom_call_target="tpu_custom_call" | custom-call | tf_op jit(solution)/shard_map/fused/pallas_call | solution.py:566
  75.3 4.2 %couple.1 = (bf16[64,256,128]{2,1,0:T(8,128)(2,1)}, bf16[2,64,256]{2,1,0:T(8,128)(2,1)}) custom-call(f32[512,256]{1,0:T(8,128)} %get-tuple-element.6.db, bf16[8,128]{1,0:T(8,128)(2,1)} %bitcast.3, bf16[2,64,256]{2,1,0:T(8,128)(2,1)} %get-tuple-element.7.hom), custom_call_target="tpu_custom_call" | custom-call | tf_op jit(solution)/shard_map/couple/pallas_call | solution.py:618
